TPU v7x, 32 devices: a whole 2x2x4 slice. The times are simulated.
32 devices in a mesh: grp: 2 (over x), tile: 16 (over z, y, core).
Axes of the slice: x: 2, y: 2, z: 4, core: 2. Of those that a mesh axis runs over, the one named last changes fastest.
Arguments:
- starting_element_condition: bfloat16 [4096, 512], P(('grp', 'tile')), parts along dimension 0, may hold values from -6 to 6
- stored_lookup_record: bfloat16 [1, 4096, 512], P(None, ('grp', 'tile')), parts along dimension 1, may hold values from -6 to 6
- stored_content_record: bfloat16 [1, 4096, 512], P(None, ('grp', 'tile')), parts along dimension 1, may hold values from -6 to 6
- scaling_multiplier_entries: float32 [512], replicated, may hold values from 0.1 to 1.9
- joint_projector_coefficients: bfloat16 [512, 1536], replicated, may hold values from -0.25 to 0.25
- final_projector: bfloat16 [512, 512], replicated, may hold values from -0.25 to 0.25
- sharpness_factor: float32 [8], replicated, may hold values from 16 to 32
- adjacent_marine_connection: int32 [32, 8], P(('grp', 'tile')), parts along dimension 0, may hold values 0 or 1
- segment_marine_marks: int32 [256], P(('grp', 'tile')), parts along dimension 0, may hold values 0 or 1
- patch_element_amounts: int32 [32], P(('grp', 'tile')), parts along dimension 0, may hold values from 32 to 128, as said below
Outputs:
- tendencies: bfloat16 [2, 4096, 512], P(None, ('grp', 'tile')), parts along dimension 1
There are 2 independent parts, one for each index of `grp`. A program takes and returns all parts, laid end to end along the dimension named above; an argument that names none is the same for every part. Nothing has to cross between parts.
Inputs may be any that keep to these rules, and one draw needn't show every extreme that they name: `adjacent_marine_connection`: 1 where the tile's water reaches the neighbour in that direction, in the order of the steps. `segment_marine_marks`: 1 for a block of sea tokens, 0 for land. `patch_element_amounts`: tokens from this position of a tile on are padding; some tile is full.
All inputs are finite; a program needn't handle non-finite values. No bound on the sum of `adjacent_marine_connection` on one device may be relied on, other than what follows from the above.
Results may differ from a plain program's by a relative error of at most 0.023.
Values may be sent and summed in bfloat16 or wider, within the bound.
A program may use at most 64 MiB of HBM per device.

v0:
```python
import jax
import jax.numpy as jnp
from jax import lax
from jax.sharding import PartitionSpec as P

HIST = 1
STEPS = 2
TW = 8


DIRECTIONS = ((-1, -1), (-1, 0), (-1, 1), (0, -1), (0, 1), (1, -1), (1, 0), (1, 1))


def passed_along(value, axis, steps):
    count = lax.axis_size(axis)
    initial, last = (max(0, -steps), min(count, count - steps))
    return lax.ppermute(value, axis, [(source, source + steps) for source in range(initial, last)])


def unit_heads(array_in, group_quantity):
    dims = array_in.shape
    per_head = array_in.astype(jnp.float32).reshape(
        dims[:-1] + (group_quantity, dims[-1] // group_quantity)
    )
    inv_rms = lax.rsqrt(jnp.mean(per_head * per_head, axis=-1, keepdims=True) + 1e-06)
    return (per_head * inv_rms).reshape(dims).astype(jnp.bfloat16)


def adjacent_focus_pass(
    request_array,
    segment_lookup_entries,
    segment_content_entries,
    lookup_permitted,
    sharpness_factor,
):
    query_rows, model_width = request_array.shape
    group_quantity = sharpness_factor.shape[0]
    channel_dimension = model_width // group_quantity
    affinity_levels = jnp.einsum(
        "qhd,khd->hqk",
        request_array.reshape(query_rows, group_quantity, channel_dimension),
        segment_lookup_entries.reshape(-1, group_quantity, channel_dimension),
        preferred_element_type=jnp.float32,
    )
    affinity_levels = affinity_levels * (sharpness_factor / channel_dimension)[:, None, None]
    weights = jnp.where(lookup_permitted[None, None, :], jnp.exp(affinity_levels), 0.0)
    denominator = jnp.sum(weights, axis=-1).T
    numerator = jnp.einsum(
        "hqk,khd->qhd",
        weights.astype(jnp.bfloat16),
        segment_content_entries.reshape(-1, group_quantity, channel_dimension),
        preferred_element_type=jnp.float32,
    )
    return (numerator.reshape(query_rows, model_width), denominator)


def body(
    starting_element_condition,
    stored_lookup_record,
    stored_content_record,
    scaling_multiplier_entries,
    joint_projector_coefficients,
    final_projector,
    sharpness_factor,
    adjacent_marine_connection,
    segment_marine_marks,
    patch_element_amounts,
):
    tok_rows, model_width = starting_element_condition.shape
    group_quantity = sharpness_factor.shape[0]
    window_len = HIST + 1
    grid_rows = lax.axis_size("tile") // TW
    tile_index = lax.axis_index("tile")
    tile_row = tile_index // TW
    tile_column = tile_index % TW
    block_count = segment_marine_marks.shape[0]
    spread = jnp.broadcast_to(
        segment_marine_marks[:, None], (block_count, tok_rows // block_count)
    ).reshape(tok_rows)
    token_ok = (spread == 1) & (jnp.arange(tok_rows) < patch_element_amounts[0])
    own_ok = jnp.tile(token_ok, window_len)
    present = []
    for direction in range(8):
        row_delta, col_delta = DIRECTIONS[direction]
        inside = (
            (tile_row + row_delta >= 0)
            & (tile_row + row_delta < grid_rows)
            & (tile_column + col_delta >= 0)
            & (tile_column + col_delta < TW)
        )
        present.append(inside & (adjacent_marine_connection[0, direction] == 1))
    past_keys = unit_heads(stored_lookup_record, group_quantity)
    spare_slots = jnp.zeros((STEPS, tok_rows, model_width), jnp.bfloat16)
    key_store = jnp.concatenate([past_keys, spare_slots], axis=0)
    value_store = jnp.concatenate([stored_content_record, spare_slots], axis=0)
    state_now = starting_element_condition
    results = []
    far_keys = []
    far_values = []
    far_ok = []
    for direction in range(8):
        row_delta, col_delta = DIRECTIONS[direction]
        offset = row_delta * TW + col_delta
        keys_in, values_in, valid_in = passed_along(
            (past_keys, stored_content_record, token_ok.astype(jnp.bfloat16)), "tile", -offset
        )
        far_keys.append(jnp.concatenate([keys_in, spare_slots], axis=0))
        far_values.append(jnp.concatenate([values_in, spare_slots], axis=0))
        far_ok.append(jnp.tile(valid_in == 1, window_len) & present[direction])
    for step_index in range(STEPS):
        widened = state_now.astype(jnp.float32)
        normed = (
            widened
            * lax.rsqrt(jnp.mean(widened * widened, axis=-1, keepdims=True) + 1e-06)
            * scaling_multiplier_entries
        ).astype(jnp.bfloat16)
        projected = jnp.dot(
            normed, joint_projector_coefficients, preferred_element_type=jnp.float32
        ).astype(jnp.bfloat16)
        request_array = unit_heads(projected[:, :model_width], group_quantity)
        new_keys = unit_heads(projected[:, model_width : 2 * model_width], group_quantity)
        request_array, new_keys, new_values = (
            request_array,
            new_keys,
            projected[:, 2 * model_width :],
        )
        key_store = key_store.at[HIST + step_index].set(new_keys)
        value_store = value_store.at[HIST + step_index].set(new_values)
        numerator, denominator = adjacent_focus_pass(
            request_array,
            key_store[step_index : step_index + window_len].reshape(-1, model_width),
            value_store[step_index : step_index + window_len].reshape(-1, model_width),
            own_ok,
            sharpness_factor,
        )
        for direction in range(8):
            row_delta, col_delta = DIRECTIONS[direction]
            offset = row_delta * TW + col_delta
            keys_in, values_in = passed_along((new_keys, new_values), "tile", -offset)
            far_keys[direction] = far_keys[direction].at[HIST + step_index].set(keys_in)
            far_values[direction] = far_values[direction].at[HIST + step_index].set(values_in)
            running_weighted_sum, running_normalizer = adjacent_focus_pass(
                request_array,
                far_keys[direction][step_index : step_index + window_len].reshape(-1, model_width),
                far_values[direction][step_index : step_index + window_len].reshape(
                    -1, model_width
                ),
                far_ok[direction],
                sharpness_factor,
            )
            numerator = numerator + running_weighted_sum
            denominator = denominator + running_normalizer
        safe_total = jnp.where(token_ok[:, None], denominator, 1.0)
        attended = (
            numerator.reshape(tok_rows, group_quantity, model_width // group_quantity)
            / safe_total[:, :, None]
        )
        attended = (
            jnp.where(token_ok[:, None, None], attended, 0.0)
            .reshape(tok_rows, model_width)
            .astype(jnp.bfloat16)
        )
        tendency = jnp.dot(attended, final_projector, preferred_element_type=jnp.float32).astype(
            jnp.bfloat16
        )
        following = (state_now.astype(jnp.float32) + tendency.astype(jnp.float32)).astype(
            jnp.bfloat16
        )
        state_now, tendency = (following, tendency)
        results.append(tendency)
    return jnp.stack(results)


def solution(mesh):
    in_specs = (
        P(("grp", "tile"), None),
        P(None, ("grp", "tile"), None),
        P(None, ("grp", "tile"), None),
        P(),
        P(),
        P(),
        P(),
        P(("grp", "tile"), None),
        P(("grp", "tile")),
        P(("grp", "tile")),
    )
    out_specs = P(None, ("grp", "tile"), None)
    return jax.shard_map(body, mesh=mesh, in_specs=in_specs, out_specs=out_specs, check_vma=False)
```

profile of v0, /device:TPU:27, one launch (start us, length us, event | category | flops | bytes accessed | tf_op | source)
XLA Modules:
  0.0 400.4 jit_solution(3780706682202395738)
XLA Ops:
  30.2 3.7 collective-permute-start.15
  35.5 2.4 collective-permute-start.17
  38.6 4.7 %collective-permute-start.22 = (bf16[128]{0:T(256)(128)(2,1)S(1)}, bf16[128]{0:T(256)(128)(2,1)S(1)}, u32[]{:S(2)}, u32[]{:S(2)}) collective-permute-start(bf16[128]{0:T(256)(128)(2,1)S(1)} %get-tuple-element.437), channel_id=1, source_target_pairs={{1,0},{2,1},{3,2},{4,3},{5,4},{6,5},{7,6},{8,7},{9,8},{10,9},{11,1... | collective-permute-start | bytes 776 | tf_op jit(solution)/shard_map/ppermute | solution.py:17
  44.1 4.1 %collective-permute-start.27 = (bf16[128]{0:T(256)(128)(2,1)S(1)}, bf16[128]{0:T(256)(128)(2,1)S(1)}, u32[]{:S(2)}, u32[]{:S(2)}) collective-permute-start(bf16[128]{0:T(256)(128)(2,1)S(1)} %get-tuple-element.437), channel_id=1, source_target_pairs={{7,0},{8,1},{9,2},{10,3},{11,4},{12,5},{13,6},{14,7},{15,8},{23,16... | collective-permute-start | bytes 776 | tf_op jit(solution)/shard_map/ppermute | solution.py:17
  48.9 5.4 %collective-permute-start.32 = (bf16[128]{0:T(256)(128)(2,1)S(1)}, bf16[128]{0:T(256)(128)(2,1)S(1)}, u32[]{:S(2)}, u32[]{:S(2)}) collective-permute-start(bf16[128]{0:T(256)(128)(2,1)S(1)} %get-tuple-element.437), channel_id=1, source_target_pairs={{8,0},{9,1},{10,2},{11,3},{12,4},{13,5},{14,6},{15,7},{24,16},{25,... | collective-permute-start | bytes 776 | tf_op jit(solution)/shard_map/ppermute | solution.py:17
  55.0 6.0 %collective-permute-start.37 = (bf16[128]{0:T(256)(128)(2,1)S(1)}, bf16[128]{0:T(256)(128)(2,1)S(1)}, u32[]{:S(2)}, u32[]{:S(2)}) collective-permute-start(bf16[128]{0:T(256)(128)(2,1)S(1)} %get-tuple-element.437), channel_id=1, source_target_pairs={{9,0},{10,1},{11,2},{12,3},{13,4},{14,5},{15,6},{25,16},{26,17},{2... | collective-permute-start | bytes 776 | tf_op jit(solution)/shard_map/ppermute | solution.py:17
  61.7 3.7 collective-permute-start.20
  65.4 4.1 %collective-permute-start.25 = (bf16[1,128,512]{2,1,0:T(8,128)(2,1)}, bf16[1,128,512]{2,1,0:T(8,128)(2,1)S(1)}, u32[]{:S(2)}, u32[]{:S(2)}) collective-permute-start(bf16[1,128,512]{2,1,0:T(8,128)(2,1)} %param.84), channel_id=1, source_target_pairs={{7,0},{8,1},{9,2},{10,3},{11,4},{12,5},{13,6},{14,7},{15,8},{23,16... | collective-permute-start | bytes 393224 | tf_op jit(solution)/shard_map/ppermute | solution.py:17
  79.2 18.8 %collective-permute-done.1 = bf16[128,512]{1,0:T(8,128)(2,1)S(1)} collective-permute-done((bf16[128,512]{1,0:T(8,128)(2,1)}, bf16[128,512]{1,0:T(8,128)(2,1)S(1)}, u32[]{:S(2)}, u32[]{:S(2)}) %collective-permute-start.1) | collective-permute-done | bytes 131104 | tf_op jit(solution)/shard_map/ppermute | solution.py:17
  99.2 6.8 %collective-permute-done.6 = bf16[128,512]{1,0:T(8,128)(2,1)S(1)} collective-permute-done((bf16[128,512]{1,0:T(8,128)(2,1)}, bf16[128,512]{1,0:T(8,128)(2,1)S(1)}, u32[]{:S(2)}, u32[]{:S(2)}) %collective-permute-start.6) | collective-permute-done | bytes 131104 | tf_op jit(solution)/shard_map/ppermute | solution.py:17
  107.3 7.9 %collective-permute-done.11 = bf16[128,512]{1,0:T(8,128)(2,1)S(1)} collective-permute-done((bf16[128,512]{1,0:T(8,128)(2,1)}, bf16[128,512]{1,0:T(8,128)(2,1)S(1)}, u32[]{:S(2)}, u32[]{:S(2)}) %collective-permute-start.11) | collective-permute-done | bytes 131104 | tf_op jit(solution)/shard_map/ppermute | solution.py:17
  115.2 3.3 collective-permute-start.16
  118.5 2.2 collective-permute-done.16
  120.7 3.8 collective-permute-start.21
  124.5 3.3 collective-permute-done.21
  129.1 3.5 collective-permute-done.26
  132.7 5.0 %collective-permute-start.31 = (bf16[128,512]{1,0:T(8,128)(2,1)}, bf16[128,512]{1,0:T(8,128)(2,1)S(1)}, u32[]{:S(2)}, u32[]{:S(2)}) collective-permute-start(bf16[128,512]{1,0:T(8,128)(2,1)} %slice.920), channel_id=1, source_target_pairs={{8,0},{9,1},{10,2},{11,3},{12,4},{13,5},{14,6},{15,7},{24,16},{25,... | collective-permute-start | bytes 393224 | tf_op jit(solution)/shard_map/ppermute | solution.py:17
  137.6 2.2 collective-permute-done.31
  144.2 4.2 %collective-permute-start.18 = (bf16[1,128,512]{1,2,0:T(8,128)(2,1)}, bf16[1,128,512]{1,2,0:T(8,128)(2,1)}, u32[]{:S(2)}, u32[]{:S(2)}) collective-permute-start(bf16[1,128,512]{1,2,0:T(8,128)(2,1)} %fusion.66), channel_id=1, source_target_pairs={{0,1},{1,2},{2,3},{3,4},{4,5},{5,6},{6,7},{7,8},{8,9},{9,10},{10,1... | collective-permute-start | bytes 393224 | tf_op jit(solution)/shard_map/ppermute | solution.py:17
  151.6 1.9 collective-permute-start.19
  155.2 2.8 collective-permute-start.23
  161.3 4.5 %collective-permute-start.24 = (bf16[128,512]{1,0:T(8,128)(2,1)}, bf16[128,512]{1,0:T(8,128)(2,1)}, u32[]{:S(2)}, u32[]{:S(2)}) collective-permute-start(bf16[128,512]{1,0:T(8,128)(2,1)} %get-tuple-element.443), channel_id=1, source_target_pairs={{1,0},{2,1},{3,2},{4,3},{5,4},{6,5},{7,6},{8,7},{9,8},{10,9},{11,1... | collective-permute-start | bytes 393224 | tf_op jit(solution)/shard_map/ppermute | solution.py:17
  167.5 6.0 %collective-permute-start.28 = (bf16[1,128,512]{1,2,0:T(8,128)(2,1)}, bf16[1,128,512]{1,2,0:T(8,128)(2,1)}, u32[]{:S(2)}, u32[]{:S(2)}) collective-permute-start(bf16[1,128,512]{1,2,0:T(8,128)(2,1)} %fusion.66), channel_id=1, source_target_pairs={{7,0},{8,1},{9,2},{10,3},{11,4},{12,5},{13,6},{14,7},{15,8},{23,16... | collective-permute-start | bytes 393224 | tf_op jit(solution)/shard_map/ppermute | solution.py:17
  176.8 1.9 collective-permute-start.29
  180.4 1.9 collective-permute-start.33
  185.7 1.9 collective-permute-start.34
  189.3 2.0 collective-permute-start.35
  194.5 1.9 collective-permute-start.36
  198.1 1.9 collective-permute-start.38
  205.0 1.8 copy.74
  214.1 1.8 copy.77
  215.9 1.8 reshape_reshape.112
  219.7 1.9 reshape_reshape.113
  222.3 1.8 copy.80
  227.2 1.8 reshape_reshape.115
  229.7 1.8 copy.83
  231.6 1.9 reshape_reshape.116
  235.4 1.8 reshape_reshape.117
  237.9 1.8 copy.86
  239.8 1.8 reshape_reshape.118
  246.1 1.8 copy.89
  251.7 1.8 reshape_reshape.121
  254.3 1.8 copy.92
  257.9 1.9 collective-permute-start.39
  263.6 1.8 reshape_reshape.123
  276.3 1.8 reshape_reshape.125
  302.1 9.0 %collective-permute-done.40 = bf16[128,512]{1,0:T(8,128)(2,1)} collective-permute-done((bf16[128,512]{1,0:T(8,128)(2,1)}, bf16[128,512]{1,0:T(8,128)(2,1)}, u32[]{:S(2)}, u32[]{:S(2)}) %collective-permute-start.40) | collective-permute-done | bytes 131104 | tf_op jit(solution)/shard_map/ppermute | solution.py:17
  314.3 6.5 %collective-permute-start.46 = (bf16[128,512]{1,0:T(8,128)(2,1)}, bf16[128,512]{1,0:T(8,128)(2,1)S(1)}, u32[]{:S(2)}, u32[]{:S(2)}) collective-permute-start(bf16[128,512]{1,0:T(8,128)(2,1)} %slice.941), channel_id=1, source_target_pairs={{0,1},{1,2},{2,3},{3,4},{4,5},{5,6},{6,7},{7,8},{8,9},{9,10},{10,1... | collective-permute-start | bytes 393224 | tf_op jit(solution)/shard_map/ppermute | solution.py:17
  321.8 4.8 %collective-permute-done.44 = bf16[128,512]{1,0:T(8,128)(2,1)} collective-permute-done((bf16[128,512]{1,0:T(8,128)(2,1)}, bf16[128,512]{1,0:T(8,128)(2,1)}, u32[]{:S(2)}, u32[]{:S(2)}) %collective-permute-start.44) | collective-permute-done | bytes 131104 | tf_op jit(solution)/shard_map/ppermute | solution.py:17
  326.6 1.9 collective-permute-start.47
  329.4 2.4 collective-permute-start.48
  331.9 1.9 collective-permute-start.49
  335.5 3.6 collective-permute-start.50
  340.8 1.9 collective-permute-start.51
  351.4 2.0 collective-permute-start.52
  355.6 2.0 collective-permute-start.53
  359.5 2.0 collective-permute-start.54
  365.2 2.2 fusion.101
  367.5 1.9 collective-permute-start.55
  370.7 2.5 fusion.100
  377.0 2.4 fusion.99
  380.7 2.8 fusion.98
  385.8 2.8 fusion.97
  389.9 2.8 fusion.96
  (478 shorter events, 183.8 us)
Async XLA Ops:
  0.0 65.4 %collective-permute-start = (bf16[1,128,512]{2,1,0:T(8,128)(2,1)}, bf16[1,128,512]{2,1,0:T(8,128)(2,1)S(1)}, u32[]{:S(2)}, u32[]{:S(2)}) collective-permute-start(bf16[1,128,512]{2,1,0:T(8,128)(2,1)} %param.84), channel_id=1, source_target_pairs={{0,9},{1,10},{2,11},{3,12},{4,13},{5,14},{6,15},{16,25},{17,26},{1... | collective-permute-start | bytes 393224 | tf_op jit(solution)/shard_map/ppermute | solution.py:17
  1.4 68.1 %collective-permute-start.5 = (bf16[1,128,512]{2,1,0:T(8,128)(2,1)}, bf16[1,128,512]{2,1,0:T(8,128)(2,1)S(1)}, u32[]{:S(2)}, u32[]{:S(2)}) collective-permute-start(bf16[1,128,512]{2,1,0:T(8,128)(2,1)} %param.84), channel_id=1, source_target_pairs={{0,8},{1,9},{2,10},{3,11},{4,12},{5,13},{6,14},{7,15},{16,24},{17,... | collective-permute-start | bytes 393224 | tf_op jit(solution)/shard_map/ppermute | solution.py:17
  4.2 23.5 %collective-permute-start.2 = (bf16[128]{0:T(256)(128)(2,1)S(1)}, bf16[128]{0:T(256)(128)(2,1)}, u32[]{:S(2)}, u32[]{:S(2)}) collective-permute-start(bf16[128]{0:T(256)(128)(2,1)S(1)} %get-tuple-element.437), channel_id=1, source_target_pairs={{0,9},{1,10},{2,11},{3,12},{4,13},{5,14},{6,15},{16,25},{17,26},{1... | collective-permute-start | bytes 776 | tf_op jit(solution)/shard_map/ppermute | solution.py:17
  5.5 24.7 %collective-permute-start.7 = (bf16[128]{0:T(256)(128)(2,1)S(1)}, bf16[128]{0:T(256)(128)(2,1)S(1)}, u32[]{:S(2)}, u32[]{:S(2)}) collective-permute-start(bf16[128]{0:T(256)(128)(2,1)S(1)} %get-tuple-element.437), channel_id=1, source_target_pairs={{0,8},{1,9},{2,10},{3,11},{4,12},{5,13},{6,14},{7,15},{16,24},{17,... | collective-permute-start | bytes 776 | tf_op jit(solution)/shard_map/ppermute | solution.py:17
  6.8 64.0 %collective-permute-start.10 = (bf16[1,128,512]{2,1,0:T(8,128)(2,1)}, bf16[1,128,512]{2,1,0:T(8,128)(2,1)S(1)}, u32[]{:S(2)}, u32[]{:S(2)}) collective-permute-start(bf16[1,128,512]{2,1,0:T(8,128)(2,1)} %param.84), channel_id=1, source_target_pairs={{0,7},{1,8},{2,9},{3,10},{4,11},{5,12},{6,13},{7,14},{8,15},{16,23... | collective-permute-start | bytes 393224 | tf_op jit(solution)/shard_map/ppermute | solution.py:17
  17.0 9.2 %copy-start.47 = (bf16[128,512]{0,1:T(8,128)(2,1)}, bf16[128,512]{0,1:T(8,128)(2,1)S(1)}, u32[]{:S(2)}) copy-start(bf16[128,512]{0,1:T(8,128)(2,1)S(1)} %copy.68) | copy-start | bytes 393220
  20.4 52.4 %copy-start.72 = (pred[256]{0:T(512)(128)(4,1)}, pred[256]{0:T(512)(128)(4,1)S(1)}, u32[]{:S(2)}) copy-start(pred[256]{0:T(512)(128)(4,1)S(1)} %broadcast_bitcast_fusion.8) | copy-start | bytes 772
  27.7 7.8 %collective-permute-start.12 = (bf16[128]{0:T(256)(128)(2,1)S(1)}, bf16[128]{0:T(256)(128)(2,1)S(1)}, u32[]{:S(2)}, u32[]{:S(2)}) collective-permute-start(bf16[128]{0:T(256)(128)(2,1)S(1)} %get-tuple-element.437), channel_id=1, source_target_pairs={{0,7},{1,8},{2,9},{3,10},{4,11},{5,12},{6,13},{7,14},{8,15},{16,23... | collective-permute-start | bytes 776 | tf_op jit(solution)/shard_map/ppermute | solution.py:17
  30.2 43.6 %collective-permute-start.15 = (bf16[1,128,512]{2,1,0:T(8,128)(2,1)}, bf16[1,128,512]{2,1,0:T(8,128)(2,1)S(1)}, u32[]{:S(2)}, u32[]{:S(2)}) collective-permute-start(bf16[1,128,512]{2,1,0:T(8,128)(2,1)} %param.84), channel_id=1, source_target_pairs={{0,1},{1,2},{2,3},{3,4},{4,5},{5,6},{6,7},{7,8},{8,9},{9,10},{10,1... | collective-permute-start | bytes 393224 | tf_op jit(solution)/shard_map/ppermute | solution.py:17
  35.5 3.1 collective-permute-start.17
  38.6 5.5 %collective-permute-start.22 = (bf16[128]{0:T(256)(128)(2,1)S(1)}, bf16[128]{0:T(256)(128)(2,1)S(1)}, u32[]{:S(2)}, u32[]{:S(2)}) collective-permute-start(bf16[128]{0:T(256)(128)(2,1)S(1)} %get-tuple-element.437), channel_id=1, source_target_pairs={{1,0},{2,1},{3,2},{4,3},{5,4},{6,5},{7,6},{8,7},{9,8},{10,9},{11,1... | collective-permute-start | bytes 776 | tf_op jit(solution)/shard_map/ppermute | solution.py:17
  44.1 4.8 %collective-permute-start.27 = (bf16[128]{0:T(256)(128)(2,1)S(1)}, bf16[128]{0:T(256)(128)(2,1)S(1)}, u32[]{:S(2)}, u32[]{:S(2)}) collective-permute-start(bf16[128]{0:T(256)(128)(2,1)S(1)} %get-tuple-element.437), channel_id=1, source_target_pairs={{7,0},{8,1},{9,2},{10,3},{11,4},{12,5},{13,6},{14,7},{15,8},{23,16... | collective-permute-start | bytes 776 | tf_op jit(solution)/shard_map/ppermute | solution.py:17
  48.9 6.1 %collective-permute-start.32 = (bf16[128]{0:T(256)(128)(2,1)S(1)}, bf16[128]{0:T(256)(128)(2,1)S(1)}, u32[]{:S(2)}, u32[]{:S(2)}) collective-permute-start(bf16[128]{0:T(256)(128)(2,1)S(1)} %get-tuple-element.437), channel_id=1, source_target_pairs={{8,0},{9,1},{10,2},{11,3},{12,4},{13,5},{14,6},{15,7},{24,16},{25,... | collective-permute-start | bytes 776 | tf_op jit(solution)/shard_map/ppermute | solution.py:17
  55.0 6.7 %collective-permute-start.37 = (bf16[128]{0:T(256)(128)(2,1)S(1)}, bf16[128]{0:T(256)(128)(2,1)S(1)}, u32[]{:S(2)}, u32[]{:S(2)}) collective-permute-start(bf16[128]{0:T(256)(128)(2,1)S(1)} %get-tuple-element.437), channel_id=1, source_target_pairs={{9,0},{10,1},{11,2},{12,3},{13,4},{14,5},{15,6},{25,16},{26,17},{2... | collective-permute-start | bytes 776 | tf_op jit(solution)/shard_map/ppermute | solution.py:17
  61.7 13.4 %collective-permute-start.20 = (bf16[1,128,512]{2,1,0:T(8,128)(2,1)}, bf16[1,128,512]{2,1,0:T(8,128)(2,1)S(1)}, u32[]{:S(2)}, u32[]{:S(2)}) collective-permute-start(bf16[1,128,512]{2,1,0:T(8,128)(2,1)} %param.84), channel_id=1, source_target_pairs={{1,0},{2,1},{3,2},{4,3},{5,4},{6,5},{7,6},{8,7},{9,8},{10,9},{11,1... | collective-permute-start | bytes 393224 | tf_op jit(solution)/shard_map/ppermute | solution.py:17
  65.4 11.0 %collective-permute-start.25 = (bf16[1,128,512]{2,1,0:T(8,128)(2,1)}, bf16[1,128,512]{2,1,0:T(8,128)(2,1)S(1)}, u32[]{:S(2)}, u32[]{:S(2)}) collective-permute-start(bf16[1,128,512]{2,1,0:T(8,128)(2,1)} %param.84), channel_id=1, source_target_pairs={{7,0},{8,1},{9,2},{10,3},{11,4},{12,5},{13,6},{14,7},{15,8},{23,16... | collective-permute-start | bytes 393224 | tf_op jit(solution)/shard_map/ppermute | solution.py:17
  69.5 8.3 %collective-permute-start.30 = (bf16[1,128,512]{2,1,0:T(8,128)(2,1)}, bf16[1,128,512]{2,1,0:T(8,128)(2,1)S(1)}, u32[]{:S(2)}, u32[]{:S(2)}) collective-permute-start(bf16[1,128,512]{2,1,0:T(8,128)(2,1)} %param.84), channel_id=1, source_target_pairs={{8,0},{9,1},{10,2},{11,3},{12,4},{13,5},{14,6},{15,7},{24,16},{25,... | collective-permute-start | bytes 393224 | tf_op jit(solution)/shard_map/ppermute | solution.py:17
  70.9 27.1 %collective-permute-start.1 = (bf16[128,512]{1,0:T(8,128)(2,1)}, bf16[128,512]{1,0:T(8,128)(2,1)S(1)}, u32[]{:S(2)}, u32[]{:S(2)}) collective-permute-start(bf16[128,512]{1,0:T(8,128)(2,1)} %slice.920), channel_id=1, source_target_pairs={{0,9},{1,10},{2,11},{3,12},{4,13},{5,14},{6,15},{16,25},{17,26},{1... | collective-permute-start | bytes 393224 | tf_op jit(solution)/shard_map/ppermute | solution.py:17
  73.8 70.4 %collective-permute-start.3 = (bf16[1,128,512]{1,2,0:T(8,128)(2,1)}, bf16[1,128,512]{1,2,0:T(8,128)(2,1)}, u32[]{:S(2)}, u32[]{:S(2)}) collective-permute-start(bf16[1,128,512]{1,2,0:T(8,128)(2,1)} %fusion.66), channel_id=1, source_target_pairs={{0,9},{1,10},{2,11},{3,12},{4,13},{5,14},{6,15},{16,25},{17,26},{1... | collective-permute-start | bytes 393224 | tf_op jit(solution)/shard_map/ppermute | solution.py:17
  75.1 66.1 %collective-permute-start.4 = (bf16[128,512]{1,0:T(8,128)(2,1)}, bf16[128,512]{1,0:T(8,128)(2,1)S(1)}, u32[]{:S(2)}, u32[]{:S(2)}) collective-permute-start(bf16[128,512]{1,0:T(8,128)(2,1)} %get-tuple-element.443), channel_id=1, source_target_pairs={{0,9},{1,10},{2,11},{3,12},{4,13},{5,14},{6,15},{16,25},{17,26},{1... | collective-permute-start | bytes 393224 | tf_op jit(solution)/shard_map/ppermute | solution.py:17
  76.5 29.6 %collective-permute-start.6 = (bf16[128,512]{1,0:T(8,128)(2,1)}, bf16[128,512]{1,0:T(8,128)(2,1)S(1)}, u32[]{:S(2)}, u32[]{:S(2)}) collective-permute-start(bf16[128,512]{1,0:T(8,128)(2,1)} %slice.920), channel_id=1, source_target_pairs={{0,8},{1,9},{2,10},{3,11},{4,12},{5,13},{6,14},{7,15},{16,24},{17,... | collective-permute-start | bytes 393224 | tf_op jit(solution)/shard_map/ppermute | solution.py:17
  77.8 77.4 %collective-permute-start.8 = (bf16[1,128,512]{1,2,0:T(8,128)(2,1)}, bf16[1,128,512]{1,2,0:T(8,128)(2,1)}, u32[]{:S(2)}, u32[]{:S(2)}) collective-permute-start(bf16[1,128,512]{1,2,0:T(8,128)(2,1)} %fusion.66), channel_id=1, source_target_pairs={{0,8},{1,9},{2,10},{3,11},{4,12},{5,13},{6,14},{7,15},{16,24},{17,... | collective-permute-start | bytes 393224 | tf_op jit(solution)/shard_map/ppermute | solution.py:17
  97.9 53.7 %collective-permute-start.9 = (bf16[128,512]{1,0:T(8,128)(2,1)}, bf16[128,512]{1,0:T(8,128)(2,1)}, u32[]{:S(2)}, u32[]{:S(2)}) collective-permute-start(bf16[128,512]{1,0:T(8,128)(2,1)} %get-tuple-element.443), channel_id=1, source_target_pairs={{0,8},{1,9},{2,10},{3,11},{4,12},{5,13},{6,14},{7,15},{16,24},{17,... | collective-permute-start | bytes 393224 | tf_op jit(solution)/shard_map/ppermute | solution.py:17
  99.2 42.0 %copy-start.6 = (bf16[3,128,512]{2,1,0:T(8,128)(2,1)}, bf16[3,128,512]{2,1,0:T(8,128)(2,1)S(1)}, u32[]{:S(2)}) copy-start(bf16[3,128,512]{2,1,0:T(8,128)(2,1)S(1)} %bitcast_dynamic-update-slice_fusion.16) | copy-start | bytes 1179652
  106.0 9.2 %collective-permute-start.11 = (bf16[128,512]{1,0:T(8,128)(2,1)}, bf16[128,512]{1,0:T(8,128)(2,1)S(1)}, u32[]{:S(2)}, u32[]{:S(2)}) collective-permute-start(bf16[128,512]{1,0:T(8,128)(2,1)} %slice.920), channel_id=1, source_target_pairs={{0,7},{1,8},{2,9},{3,10},{4,11},{5,12},{6,13},{7,14},{8,15},{16,23... | collective-permute-start | bytes 393224 | tf_op jit(solution)/shard_map/ppermute | solution.py:17
  107.3 33.8 %copy-start.4 = (bf16[3,128,512]{2,1,0:T(8,128)(2,1)}, bf16[3,128,512]{2,1,0:T(8,128)(2,1)S(1)}, u32[]{:S(2)}) copy-start(bf16[3,128,512]{2,1,0:T(8,128)(2,1)S(1)} %bitcast_dynamic-update-slice_fusion.15) | copy-start | bytes 1179652
  115.2 5.5 %collective-permute-start.16 = (bf16[128,512]{1,0:T(8,128)(2,1)}, bf16[128,512]{1,0:T(8,128)(2,1)S(1)}, u32[]{:S(2)}, u32[]{:S(2)}) collective-permute-start(bf16[128,512]{1,0:T(8,128)(2,1)} %slice.920), channel_id=1, source_target_pairs={{0,1},{1,2},{2,3},{3,4},{4,5},{5,6},{6,7},{7,8},{8,9},{9,10},{10,1... | collective-permute-start | bytes 393224 | tf_op jit(solution)/shard_map/ppermute | solution.py:17
  118.5 103.1 %copy-start.2 = (bf16[3,128,512]{2,1,0:T(8,128)(2,1)}, bf16[3,128,512]{2,1,0:T(8,128)(2,1)S(1)}, u32[]{:S(2)}) copy-start(bf16[3,128,512]{2,1,0:T(8,128)(2,1)S(1)} %bitcast_dynamic-update-slice_fusion.14) | copy-start | bytes 1179652
  120.7 7.1 %collective-permute-start.21 = (bf16[128,512]{1,0:T(8,128)(2,1)}, bf16[128,512]{1,0:T(8,128)(2,1)S(1)}, u32[]{:S(2)}, u32[]{:S(2)}) collective-permute-start(bf16[128,512]{1,0:T(8,128)(2,1)} %slice.920), channel_id=1, source_target_pairs={{1,0},{2,1},{3,2},{4,3},{5,4},{6,5},{7,6},{8,7},{9,8},{10,9},{11,1... | collective-permute-start | bytes 393224 | tf_op jit(solution)/shard_map/ppermute | solution.py:17
  127.8 4.8 %collective-permute-start.26 = (bf16[128,512]{1,0:T(8,128)(2,1)}, bf16[128,512]{1,0:T(8,128)(2,1)S(1)}, u32[]{:S(2)}, u32[]{:S(2)}) collective-permute-start(bf16[128,512]{1,0:T(8,128)(2,1)} %slice.920), channel_id=1, source_target_pairs={{7,0},{8,1},{9,2},{10,3},{11,4},{12,5},{13,6},{14,7},{15,8},{23,16... | collective-permute-start | bytes 393224 | tf_op jit(solution)/shard_map/ppermute | solution.py:17
  132.7 7.2 %collective-permute-start.31 = (bf16[128,512]{1,0:T(8,128)(2,1)}, bf16[128,512]{1,0:T(8,128)(2,1)S(1)}, u32[]{:S(2)}, u32[]{:S(2)}) collective-permute-start(bf16[128,512]{1,0:T(8,128)(2,1)} %slice.920), channel_id=1, source_target_pairs={{8,0},{9,1},{10,2},{11,3},{12,4},{13,5},{14,6},{15,7},{24,16},{25,... | collective-permute-start | bytes 393224 | tf_op jit(solution)/shard_map/ppermute | solution.py:17
  139.9 27.6 %collective-permute-start.13 = (bf16[1,128,512]{1,2,0:T(8,128)(2,1)}, bf16[1,128,512]{1,2,0:T(8,128)(2,1)}, u32[]{:S(2)}, u32[]{:S(2)}) collective-permute-start(bf16[1,128,512]{1,2,0:T(8,128)(2,1)} %fusion.66), channel_id=1, source_target_pairs={{0,7},{1,8},{2,9},{3,10},{4,11},{5,12},{6,13},{7,14},{8,15},{16,23... | collective-permute-start | bytes 393224 | tf_op jit(solution)/shard_map/ppermute | solution.py:17
  141.2 20.1 %collective-permute-start.14 = (bf16[128,512]{1,0:T(8,128)(2,1)}, bf16[128,512]{1,0:T(8,128)(2,1)}, u32[]{:S(2)}, u32[]{:S(2)}) collective-permute-start(bf16[128,512]{1,0:T(8,128)(2,1)} %get-tuple-element.443), channel_id=1, source_target_pairs={{0,7},{1,8},{2,9},{3,10},{4,11},{5,12},{6,13},{7,14},{8,15},{16,23... | collective-permute-start | bytes 393224 | tf_op jit(solution)/shard_map/ppermute | solution.py:17
  144.2 36.2 %collective-permute-start.18 = (bf16[1,128,512]{1,2,0:T(8,128)(2,1)}, bf16[1,128,512]{1,2,0:T(8,128)(2,1)}, u32[]{:S(2)}, u32[]{:S(2)}) collective-permute-start(bf16[1,128,512]{1,2,0:T(8,128)(2,1)} %fusion.66), channel_id=1, source_target_pairs={{0,1},{1,2},{2,3},{3,4},{4,5},{5,6},{6,7},{7,8},{8,9},{9,10},{10,1... | collective-permute-start | bytes 393224 | tf_op jit(solution)/shard_map/ppermute | solution.py:17
  151.6 25.2 %collective-permute-start.19 = (bf16[128,512]{1,0:T(8,128)(2,1)}, bf16[128,512]{1,0:T(8,128)(2,1)}, u32[]{:S(2)}, u32[]{:S(2)}) collective-permute-start(bf16[128,512]{1,0:T(8,128)(2,1)} %get-tuple-element.443), channel_id=1, source_target_pairs={{0,1},{1,2},{2,3},{3,4},{4,5},{5,6},{6,7},{7,8},{8,9},{9,10},{10,1... | collective-permute-start | bytes 393224 | tf_op jit(solution)/shard_map/ppermute | solution.py:17
  155.2 34.1 %collective-permute-start.23 = (bf16[1,128,512]{1,2,0:T(8,128)(2,1)}, bf16[1,128,512]{1,2,0:T(8,128)(2,1)}, u32[]{:S(2)}, u32[]{:S(2)}) collective-permute-start(bf16[1,128,512]{1,2,0:T(8,128)(2,1)} %fusion.66), channel_id=1, source_target_pairs={{1,0},{2,1},{3,2},{4,3},{5,4},{6,5},{7,6},{8,7},{9,8},{10,9},{11,1... | collective-permute-start | bytes 393224 | tf_op jit(solution)/shard_map/ppermute | solution.py:17
  161.3 24.4 %collective-permute-start.24 = (bf16[128,512]{1,0:T(8,128)(2,1)}, bf16[128,512]{1,0:T(8,128)(2,1)}, u32[]{:S(2)}, u32[]{:S(2)}) collective-permute-start(bf16[128,512]{1,0:T(8,128)(2,1)} %get-tuple-element.443), channel_id=1, source_target_pairs={{1,0},{2,1},{3,2},{4,3},{5,4},{6,5},{7,6},{8,7},{9,8},{10,9},{11,1... | collective-permute-start | bytes 393224 | tf_op jit(solution)/shard_map/ppermute | solution.py:17
  167.5 30.6 %collective-permute-start.28 = (bf16[1,128,512]{1,2,0:T(8,128)(2,1)}, bf16[1,128,512]{1,2,0:T(8,128)(2,1)}, u32[]{:S(2)}, u32[]{:S(2)}) collective-permute-start(bf16[1,128,512]{1,2,0:T(8,128)(2,1)} %fusion.66), channel_id=1, source_target_pairs={{7,0},{8,1},{9,2},{10,3},{11,4},{12,5},{13,6},{14,7},{15,8},{23,16... | collective-permute-start | bytes 393224 | tf_op jit(solution)/shard_map/ppermute | solution.py:17
  176.8 17.7 %collective-permute-start.29 = (bf16[128,512]{1,0:T(8,128)(2,1)}, bf16[128,512]{1,0:T(8,128)(2,1)}, u32[]{:S(2)}, u32[]{:S(2)}) collective-permute-start(bf16[128,512]{1,0:T(8,128)(2,1)} %get-tuple-element.443), channel_id=1, source_target_pairs={{7,0},{8,1},{9,2},{10,3},{11,4},{12,5},{13,6},{14,7},{15,8},{23,16... | collective-permute-start | bytes 393224 | tf_op jit(solution)/shard_map/ppermute | solution.py:17
  180.4 80.5 %collective-permute-start.33 = (bf16[1,128,512]{1,2,0:T(8,128)(2,1)}, bf16[1,128,512]{1,2,0:T(8,128)(2,1)}, u32[]{:S(2)}, u32[]{:S(2)}) collective-permute-start(bf16[1,128,512]{1,2,0:T(8,128)(2,1)} %fusion.66), channel_id=1, source_target_pairs={{8,0},{9,1},{10,2},{11,3},{12,4},{13,5},{14,6},{15,7},{24,16},{25,... | collective-permute-start | bytes 393224 | tf_op jit(solution)/shard_map/ppermute | solution.py:17
  185.7 72.3 %collective-permute-start.34 = (bf16[128,512]{1,0:T(8,128)(2,1)}, bf16[128,512]{1,0:T(8,128)(2,1)}, u32[]{:S(2)}, u32[]{:S(2)}) collective-permute-start(bf16[128,512]{1,0:T(8,128)(2,1)} %get-tuple-element.443), channel_id=1, source_target_pairs={{8,0},{9,1},{10,2},{11,3},{12,4},{13,5},{14,6},{15,7},{24,16},{25,... | collective-permute-start | bytes 393224 | tf_op jit(solution)/shard_map/ppermute | solution.py:17
  189.3 76.2 %collective-permute-start.35 = (bf16[1,128,512]{2,1,0:T(8,128)(2,1)}, bf16[1,128,512]{2,1,0:T(8,128)(2,1)}, u32[]{:S(2)}, u32[]{:S(2)}) collective-permute-start(bf16[1,128,512]{2,1,0:T(8,128)(2,1)} %param.84), channel_id=1, source_target_pairs={{9,0},{10,1},{11,2},{12,3},{13,4},{14,5},{15,6},{25,16},{26,17},{2... | collective-permute-start | bytes 393224 | tf_op jit(solution)/shard_map/ppermute | solution.py:17
  194.5 71.9 %collective-permute-start.36 = (bf16[128,512]{1,0:T(8,128)(2,1)}, bf16[128,512]{1,0:T(8,128)(2,1)}, u32[]{:S(2)}, u32[]{:S(2)}) collective-permute-start(bf16[128,512]{1,0:T(8,128)(2,1)} %slice.920), channel_id=1, source_target_pairs={{9,0},{10,1},{11,2},{12,3},{13,4},{14,5},{15,6},{25,16},{26,17},{2... | collective-permute-start | bytes 393224 | tf_op jit(solution)/shard_map/ppermute | solution.py:17
  198.1 75.4 %collective-permute-start.38 = (bf16[1,128,512]{1,2,0:T(8,128)(2,1)}, bf16[1,128,512]{1,2,0:T(8,128)(2,1)}, u32[]{:S(2)}, u32[]{:S(2)}) collective-permute-start(bf16[1,128,512]{1,2,0:T(8,128)(2,1)} %fusion.66), channel_id=1, source_target_pairs={{9,0},{10,1},{11,2},{12,3},{13,4},{14,5},{15,6},{25,16},{26,17},{2... | collective-permute-start | bytes 393224 | tf_op jit(solution)/shard_map/ppermute | solution.py:17
  257.9 14.5 %collective-permute-start.39 = (bf16[128,512]{1,0:T(8,128)(2,1)}, bf16[128,512]{1,0:T(8,128)(2,1)}, u32[]{:S(2)}, u32[]{:S(2)}) collective-permute-start(bf16[128,512]{1,0:T(8,128)(2,1)} %get-tuple-element.443), channel_id=1, source_target_pairs={{9,0},{10,1},{11,2},{12,3},{13,4},{14,5},{15,6},{25,16},{26,17},{2... | collective-permute-start | bytes 393224 | tf_op jit(solution)/shard_map/ppermute | solution.py:17
  289.6 21.5 %collective-permute-start.40 = (bf16[128,512]{1,0:T(8,128)(2,1)}, bf16[128,512]{1,0:T(8,128)(2,1)}, u32[]{:S(2)}, u32[]{:S(2)}) collective-permute-start(bf16[128,512]{1,0:T(8,128)(2,1)} %slice.941), channel_id=1, source_target_pairs={{0,9},{1,10},{2,11},{3,12},{4,13},{5,14},{6,15},{16,25},{17,26},{1... | collective-permute-start | bytes 393224 | tf_op jit(solution)/shard_map/ppermute | solution.py:17
  290.9 23.4 %collective-permute-start.42 = (bf16[128,512]{1,0:T(8,128)(2,1)}, bf16[128,512]{1,0:T(8,128)(2,1)}, u32[]{:S(2)}, u32[]{:S(2)}) collective-permute-start(bf16[128,512]{1,0:T(8,128)(2,1)} %slice.941), channel_id=1, source_target_pairs={{0,8},{1,9},{2,10},{3,11},{4,12},{5,13},{6,14},{7,15},{16,24},{17,... | collective-permute-start | bytes 393224 | tf_op jit(solution)/shard_map/ppermute | solution.py:17
  293.6 38.3 %collective-permute-start.41 = (bf16[128,512]{1,0:T(8,128)(2,1)}, bf16[128,512]{1,0:T(8,128)(2,1)}, u32[]{:S(2)}, u32[]{:S(2)}) collective-permute-start(bf16[128,512]{1,0:T(8,128)(2,1)} %get-tuple-element.439), channel_id=1, source_target_pairs={{0,9},{1,10},{2,11},{3,12},{4,13},{5,14},{6,15},{16,25},{17,26},{1... | collective-permute-start | bytes 393224 | tf_op jit(solution)/shard_map/ppermute | solution.py:17
  294.9 40.6 %collective-permute-start.43 = (bf16[128,512]{1,0:T(8,128)(2,1)}, bf16[128,512]{1,0:T(8,128)(2,1)}, u32[]{:S(2)}, u32[]{:S(2)}) collective-permute-start(bf16[128,512]{1,0:T(8,128)(2,1)} %get-tuple-element.439), channel_id=1, source_target_pairs={{0,8},{1,9},{2,10},{3,11},{4,12},{5,13},{6,14},{7,15},{16,24},{17,... | collective-permute-start | bytes 393224 | tf_op jit(solution)/shard_map/ppermute | solution.py:17
  296.2 30.4 %collective-permute-start.44 = (bf16[128,512]{1,0:T(8,128)(2,1)}, bf16[128,512]{1,0:T(8,128)(2,1)}, u32[]{:S(2)}, u32[]{:S(2)}) collective-permute-start(bf16[128,512]{1,0:T(8,128)(2,1)} %slice.941), channel_id=1, source_target_pairs={{0,7},{1,8},{2,9},{3,10},{4,11},{5,12},{6,13},{7,14},{8,15},{16,23... | collective-permute-start | bytes 393224 | tf_op jit(solution)/shard_map/ppermute | solution.py:17
  300.4 12.0 %copy-start.7 = (bf16[3,128,512]{2,1,0:T(8,128)(2,1)S(1)}, bf16[3,128,512]{2,1,0:T(8,128)(2,1)}, u32[]{:S(2)}) copy-start(bf16[3,128,512]{2,1,0:T(8,128)(2,1)} %copy-done.6) | copy-start | bytes 1179652
  300.6 20.3 %copy-start.5 = (bf16[3,128,512]{2,1,0:T(8,128)(2,1)S(1)}, bf16[3,128,512]{2,1,0:T(8,128)(2,1)}, u32[]{:S(2)}) copy-start(bf16[3,128,512]{2,1,0:T(8,128)(2,1)} %copy-done.4) | copy-start | bytes 1179652
  300.6 27.9 %copy-start.3 = (bf16[3,128,512]{2,1,0:T(8,128)(2,1)S(1)}, bf16[3,128,512]{2,1,0:T(8,128)(2,1)}, u32[]{:S(2)}) copy-start(bf16[3,128,512]{2,1,0:T(8,128)(2,1)} %copy-done.2) | copy-start | bytes 1179652
  311.1 29.7 %collective-permute-start.45 = (bf16[128,512]{1,0:T(8,128)(2,1)}, bf16[128,512]{1,0:T(8,128)(2,1)S(1)}, u32[]{:S(2)}, u32[]{:S(2)}) collective-permute-start(bf16[128,512]{1,0:T(8,128)(2,1)} %get-tuple-element.439), channel_id=1, source_target_pairs={{0,7},{1,8},{2,9},{3,10},{4,11},{5,12},{6,13},{7,14},{8,15},{16,23... | collective-permute-start | bytes 393224 | tf_op jit(solution)/shard_map/ppermute | solution.py:17
  314.3 15.1 %collective-permute-start.46 = (bf16[128,512]{1,0:T(8,128)(2,1)}, bf16[128,512]{1,0:T(8,128)(2,1)S(1)}, u32[]{:S(2)}, u32[]{:S(2)}) collective-permute-start(bf16[128,512]{1,0:T(8,128)(2,1)} %slice.941), channel_id=1, source_target_pairs={{0,1},{1,2},{2,3},{3,4},{4,5},{5,6},{6,7},{7,8},{8,9},{9,10},{10,1... | collective-permute-start | bytes 393224 | tf_op jit(solution)/shard_map/ppermute | solution.py:17
  326.6 24.8 %collective-permute-start.47 = (bf16[128,512]{1,0:T(8,128)(2,1)}, bf16[128,512]{1,0:T(8,128)(2,1)S(1)}, u32[]{:S(2)}, u32[]{:S(2)}) collective-permute-start(bf16[128,512]{1,0:T(8,128)(2,1)} %get-tuple-element.439), channel_id=1, source_target_pairs={{0,1},{1,2},{2,3},{3,4},{4,5},{5,6},{6,7},{7,8},{8,9},{9,10},{10,1... | collective-permute-start | bytes 393224 | tf_op jit(solution)/shard_map/ppermute | solution.py:17
  329.4 26.2 %collective-permute-start.48 = (bf16[128,512]{1,0:T(8,128)(2,1)}, bf16[128,512]{1,0:T(8,128)(2,1)S(1)}, u32[]{:S(2)}, u32[]{:S(2)}) collective-permute-start(bf16[128,512]{1,0:T(8,128)(2,1)} %slice.941), channel_id=1, source_target_pairs={{1,0},{2,1},{3,2},{4,3},{5,4},{6,5},{7,6},{8,7},{9,8},{10,9},{11,1... | collective-permute-start | bytes 393224 | tf_op jit(solution)/shard_map/ppermute | solution.py:17
  331.9 27.6 %collective-permute-start.49 = (bf16[128,512]{1,0:T(8,128)(2,1)}, bf16[128,512]{1,0:T(8,128)(2,1)}, u32[]{:S(2)}, u32[]{:S(2)}) collective-permute-start(bf16[128,512]{1,0:T(8,128)(2,1)} %get-tuple-element.439), channel_id=1, source_target_pairs={{1,0},{2,1},{3,2},{4,3},{5,4},{6,5},{7,6},{8,7},{9,8},{10,9},{11,1... | collective-permute-start | bytes 393224 | tf_op jit(solution)/shard_map/ppermute | solution.py:17
  335.5 32.0 %collective-permute-start.50 = (bf16[128,512]{1,0:T(8,128)(2,1)}, bf16[128,512]{1,0:T(8,128)(2,1)}, u32[]{:S(2)}, u32[]{:S(2)}) collective-permute-start(bf16[128,512]{1,0:T(8,128)(2,1)} %slice.941), channel_id=1, source_target_pairs={{7,0},{8,1},{9,2},{10,3},{11,4},{12,5},{13,6},{14,7},{15,8},{23,16... | collective-permute-start | bytes 393224 | tf_op jit(solution)/shard_map/ppermute | solution.py:17
  340.8 32.4 %collective-permute-start.51 = (bf16[128,512]{1,0:T(8,128)(2,1)}, bf16[128,512]{1,0:T(8,128)(2,1)}, u32[]{:S(2)}, u32[]{:S(2)}) collective-permute-start(bf16[128,512]{1,0:T(8,128)(2,1)} %get-tuple-element.439), channel_id=1, source_target_pairs={{7,0},{8,1},{9,2},{10,3},{11,4},{12,5},{13,6},{14,7},{15,8},{23,16... | collective-permute-start | bytes 393224 | tf_op jit(solution)/shard_map/ppermute | solution.py:17
  351.4 28.0 %collective-permute-start.52 = (bf16[128,512]{1,0:T(8,128)(2,1)}, bf16[128,512]{1,0:T(8,128)(2,1)}, u32[]{:S(2)}, u32[]{:S(2)}) collective-permute-start(bf16[128,512]{1,0:T(8,128)(2,1)} %slice.941), channel_id=1, source_target_pairs={{8,0},{9,1},{10,2},{11,3},{12,4},{13,5},{14,6},{15,7},{24,16},{25,... | collective-permute-start | bytes 393224 | tf_op jit(solution)/shard_map/ppermute | solution.py:17
  355.6 27.9 %collective-permute-start.53 = (bf16[128,512]{1,0:T(8,128)(2,1)}, bf16[128,512]{1,0:T(8,128)(2,1)}, u32[]{:S(2)}, u32[]{:S(2)}) collective-permute-start(bf16[128,512]{1,0:T(8,128)(2,1)} %get-tuple-element.439), channel_id=1, source_target_pairs={{8,0},{9,1},{10,2},{11,3},{12,4},{13,5},{14,6},{15,7},{24,16},{25,... | collective-permute-start | bytes 393224 | tf_op jit(solution)/shard_map/ppermute | solution.py:17
  359.5 29.1 %collective-permute-start.54 = (bf16[128,512]{1,0:T(8,128)(2,1)}, bf16[128,512]{1,0:T(8,128)(2,1)}, u32[]{:S(2)}, u32[]{:S(2)}) collective-permute-start(bf16[128,512]{1,0:T(8,128)(2,1)} %slice.941), channel_id=1, source_target_pairs={{9,0},{10,1},{11,2},{12,3},{13,4},{14,5},{15,6},{25,16},{26,17},{2... | collective-permute-start | bytes 393224 | tf_op jit(solution)/shard_map/ppermute | solution.py:17
  367.5 25.2 %collective-permute-start.55 = (bf16[128,512]{1,0:T(8,128)(2,1)}, bf16[128,512]{1,0:T(8,128)(2,1)}, u32[]{:S(2)}, u32[]{:S(2)}) collective-permute-start(bf16[128,512]{1,0:T(8,128)(2,1)} %get-tuple-element.439), channel_id=1, source_target_pairs={{9,0},{10,1},{11,2},{12,3},{13,4},{14,5},{15,6},{25,16},{26,17},{2... | collective-permute-start | bytes 393224 | tf_op jit(solution)/shard_map/ppermute | solution.py:17
  (66 other events, 159.8 us)
where the time goes:
time: 404 us; the launch traced here: 400 us
  local copies, waits for them, and re-layouts  156 us (39%)
  starting transfers between devices  135 us (33%)
  waiting for transfers between devices  61.5 us (15%)
  matrix products  33.7 us (8%)
  between operations  8.3 us (2%)
  other arithmetic  6.09 us (2%)
    ppermute x56, starting transfers between devices, passed_along(): lax.ppermute(value, axis, [(source, source + steps) for source in range(i...  135 us
    ppermute x56, waiting for transfers between devices, passed_along(): lax.ppermute(value, axis, [(source, source + steps) for source in range(i...  61.5 us
    dot_general x18, matrix products, adjacent_focus_pass(): jnp.einsum('qhd,khd->hqk', request_array.reshape(query_rows, group_quanti...  24.6 us
    slice x32, local copies, waits for them, and re-layouts, body(): far_values[direction][step_index:step_index + window_len]  23.8 us
    slice x32, local copies, waits for them, and re-layouts, body(): far_keys[direction][step_index:step_index + window_len]  21.7 us
    another operation x18, local copies, waits for them, and re-layouts, adjacent_focus_pass(): segment_lookup_entries.reshape(-1, group_quantity, channel_dimension)  20.6 us
    another operation x18, local copies, waits for them, and re-layouts  20.5 us
    another operation x18, local copies, waits for them, and re-layouts, adjacent_focus_pass(): segment_content_entries.reshape(-1, group_quantity, channel_dimension)  15.6 us
  transfers between devices with their start and end apart: 56, of which 16 were waited for; matrix products, arithmetic and copies ran while one was open for 43% of the time, Pallas kernels for 0%

commit v1 on v0

v1 whole, which is shorter than its diff:
```python
import functools

import jax
import jax.numpy as jnp
from jax import lax
from jax.experimental import pallas as pl
from jax.experimental.pallas import tpu as pltpu
from jax.sharding import PartitionSpec as P

TW = 8
STEPS = 2
LOG2E = 1.4426950408889634
NT = (((1,), (1,)), ((), ()))
DIRECTIONS = ((-1, -1), (-1, 0), (-1, 1), (0, -1), (0, 1), (1, -1), (1, 0), (1, 1))


def dot(a, b):
    return jnp.dot(a, b, preferred_element_type=jnp.float32)


def kernel(
    tiles,
    x_ref,
    k_ref,
    v_ref,
    gain_ref,
    w_ref,
    wo_ref,
    sharp_ref,
    adj_ref,
    marks_ref,
    amount_ref,
    out_ref,
    gx,
    gk,
    gv,
    gx1,
    ks,
    vs,
    ms,
    qs,
    acc,
    ones_s,
    send_v,
    recv_v,
    send_h,
    recv_h,
):
    tok, width = x_ref.shape
    heads = sharp_ref.shape[0]
    hd = width // heads
    rows = tiles // TW
    t = lax.axis_index("tile")
    row = t // TW
    col = t % TW
    two = rows == 2
    groups = 2 if two else 3
    has_left = col > 0
    has_right = col < TW - 1
    if two:
        verticals = [(1, 1, None, jnp.where(row == 0, t + TW, t - TW))]
    else:
        verticals = [
            (1, 2, row > 0, jnp.maximum(t - TW, 0)),
            (2, 1, row < rows - 1, jnp.minimum(t + TW, tiles - 1)),
        ]
    sides = [
        (has_right, jnp.minimum(t + 1, tiles - 1), has_left),
        (has_left, jnp.maximum(t - 1, 0), has_right),
    ]
    group_on = [None] + [v[2] for v in verticals]

    def when(*conds):
        conds = [c for c in conds if c is not None]
        if not conds:
            return lambda f: f()
        c = conds[0]
        for d in conds[1:]:
            c = jnp.logical_and(c, d)
        return pl.when(c)

    bufs = [gx, gk, gv, gx1]

    def vcopy(chunk, i):
        here, there, _, dev = verticals[i]
        return pltpu.make_async_remote_copy(
            src_ref=bufs[chunk].at[0, 0],
            dst_ref=bufs[chunk].at[there, 0],
            send_sem=send_v.at[chunk, there],
            recv_sem=recv_v.at[chunk, there],
            device_id={"tile": dev},
            device_id_type=pl.DeviceIdType.MESH,
        )

    def vwait(chunk, i):
        here, _, _, dev = verticals[i]
        pltpu.make_async_remote_copy(
            src_ref=bufs[chunk].at[0, 0],
            dst_ref=bufs[chunk].at[here, 0],
            send_sem=send_v.at[chunk, here],
            recv_sem=recv_v.at[chunk, here],
            device_id={"tile": dev},
            device_id_type=pl.DeviceIdType.MESH,
        ).wait_recv()

    def hcopy(chunk, g, side):
        return pltpu.make_async_remote_copy(
            src_ref=bufs[chunk].at[g, 0],
            dst_ref=bufs[chunk].at[g, 1 + side],
            send_sem=send_h.at[chunk, g, side],
            recv_sem=recv_h.at[chunk, g, side],
            device_id={"tile": sides[side][1]},
            device_id_type=pl.DeviceIdType.MESH,
        )

    barrier = pltpu.get_barrier_semaphore()
    reach = [(v[2], v[3]) for v in verticals] + [(s[0], s[1]) for s in sides]
    for on, dev in reach:

        @when(on)
        def _(dev=dev):
            pl.semaphore_signal(
                barrier, inc=1, device_id={"tile": dev}, device_id_type=pl.DeviceIdType.MESH
            )

    blocks = marks_ref.shape[0]
    per = tok // blocks

    def validity(pos):
        m = jnp.zeros(pos.shape, jnp.int32)
        for b in range(blocks):
            m = jnp.where((pos >= b * per) & (pos < (b + 1) * per), marks_ref[b], m)
        return (m == 1) & (pos < amount_ref[0])

    ri = lax.broadcasted_iota(jnp.int32, (tok, tok), 0)
    ci = lax.broadcasted_iota(jnp.int32, (tok, tok), 1)
    ok = validity(ri)
    gx[0, 0, :tok, :] = x_ref[...]
    gx[0, 0, tok:, :] = jnp.zeros((16, width), jnp.bfloat16)
    gx[0, 0, tok:, :tok] = jnp.where(
        validity(lax.broadcasted_iota(jnp.int32, (16, tok), 1)), 1.0, 0.0
    ).astype(jnp.bfloat16)
    gv[0, 0] = v_ref[0]
    qw = 4 * hd
    e0 = lax.broadcasted_iota(jnp.int32, (qw, qw), 0) >> 6
    e1 = lax.broadcasted_iota(jnp.int32, (qw, qw), 1) >> 6
    ones_s[...] = jnp.where(e0 == e1, 1.0 / hd, 0.0).astype(jnp.bfloat16)

    peers = 0
    for on, dev in reach:
        peers = peers + (1 if on is None else on.astype(jnp.int32))
    pl.semaphore_wait(barrier, peers)

    def start_vertical(chunk):
        for i, v in enumerate(verticals):

            @when(v[2])
            def _(i=i):
                vcopy(chunk, i).start()

    def start_sides(chunk, g):
        for side in range(2):

            @when(sides[side][0], group_on[g])
            def _(side=side):
                hcopy(chunk, g, side).start()

    def unit(u):
        f = u.astype(jnp.float32)
        sq = (f * f).astype(jnp.bfloat16)
        mean = jnp.concatenate(
            [dot(sq[:, i : i + qw], ones_s[...]) for i in range(0, width, qw)], axis=1
        )
        return f * lax.rsqrt(mean + 1e-06)

    start_vertical(0)
    start_vertical(2)
    start_sides(0, 0)
    start_sides(2, 0)
    gk[0, 0] = unit(k_ref[0]).astype(jnp.bfloat16)
    start_vertical(1)
    start_sides(1, 0)

    lane = lax.broadcasted_iota(jnp.int32, (1, width), 1)
    scale = jnp.zeros((1, width), jnp.float32)
    for h in range(heads):
        scale = jnp.where(
            (lane >= h * hd) & (lane < (h + 1) * hd), sharp_ref[h] * (LOG2E / hd), scale
        )

    def norm(x):
        f = x.astype(jnp.float32)
        r = lax.rsqrt(jnp.mean(f * f, axis=-1, keepdims=True) + 1e-06)
        return (f * r * gain_ref[...]).astype(jnp.bfloat16)

    def slot_of(g, c):
        return g * 3 + c

    def present(g, c):
        dc = (0, -1, 1)[c]

        def adj(dr):
            return adj_ref[0, DIRECTIONS.index((dr, dc))]

        if g == 0:
            return None if c == 0 else adj(0)
        if two:
            return jnp.where(row == 0, adj(1), adj(-1))
        return adj(-1) if g == 1 else adj(1)

    quads = width // qw

    def attend(s, g, c, first):
        n = slot_of(g, c)
        m = ms[n]
        for q in range(quads):
            keys = ks[n, s * tok : (s + 2) * tok, q * qw : (q + 1) * qw]
            scores = lax.dot_general(qs[q], keys, NT, preferred_element_type=jnp.float32)
            p = jnp.exp2(scores).astype(jnp.bfloat16)
            for a in range(2):
                pair = q * 2 + a
                vals = vs[n, s * tok : (s + 2) * tok, pair * 2 * hd : (pair + 1) * 2 * hd]
                r = dot(p[a * 2 * tok : (a + 1) * 2 * tok], jnp.concatenate([vals, m], axis=1))
                if first:
                    acc[pair] = r
                else:
                    acc[pair] += r

    def project(s, g, c, x):
        n = slot_of(g, c)
        kv = dot(norm(x), w_ref[:, width:]).astype(jnp.bfloat16)
        base = (s + 1) * tok
        ks[n, base : base + tok, :] = unit(kv[:, :width]).astype(jnp.bfloat16)
        m = ms[n, :tok, :1].astype(jnp.float32)
        vs[n, base : base + tok, :] = (kv[:, width:].astype(jnp.float32) * m).astype(
            jnp.bfloat16
        )

    def prepare(g, c):
        n = slot_of(g, c)
        line = gx[g, c, tok : tok + 16, :tok].astype(jnp.float32)[:1]
        m = jnp.sum(jnp.where(ri == ci, line, 0.0), axis=1, keepdims=True)
        seen = present(g, c)
        if seen is not None:
            m = m * jnp.where(seen == 1, 1.0, 0.0)
        mb = jnp.broadcast_to(m, (tok, 2 * hd)).astype(jnp.bfloat16)
        ms[n, :tok, :] = mb
        ms[n, tok:, :] = mb
        ks[n, :tok, :] = gk[g, c]
        vs[n, :tok, :] = (gv[g, c].astype(jnp.float32) * m).astype(jnp.bfloat16)

    def source(s, g, c, first=False):
        if s == 0:
            prepare(g, c)
            project(s, g, c, gx[g, c, :tok, :])
        else:
            project(s, g, c, gx1[g, c])
        attend(s, g, c, first)

    for s in range(STEPS):
        chunks = (0, 2, 1) if s == 0 else (3,)
        x = x_ref[...] if s == 0 else gx1[0, 0]
        if s == 1:
            start_vertical(3)
            start_sides(3, 0)
        u = dot(norm(x), w_ref[:, :width]).astype(jnp.bfloat16)
        query = unit(u) * scale
        for q in range(quads):
            part = query[:, q * qw : (q + 1) * qw]
            lanes = lax.broadcasted_iota(jnp.int32, (tok, qw), 1)
            for a in range(4):
                qs[q, a * tok : (a + 1) * tok, :] = jnp.where(
                    (lanes >= a * hd) & (lanes < (a + 1) * hd), part, 0.0
                ).astype(jnp.bfloat16)
        source(s, 0, 0, True)

        def from_side(g, side):
            @when(sides[side][2], group_on[g])
            def _():
                for chunk in chunks:
                    hcopy(chunk, g, side).wait_recv()
                source(s, g, 1 + side)

        from_side(0, 0)
        from_side(0, 1)
        for i, v in enumerate(verticals):
            g = v[0]
            for chunk in chunks:

                @when(v[2])
                def _(chunk=chunk, i=i):
                    vwait(chunk, i)

                start_sides(chunk, g)

            @when(v[2])
            def _(g=g):
                source(s, g, 0)

        for v in verticals:
            from_side(v[0], 0)
            from_side(v[0], 1)
        half = lax.broadcasted_iota(jnp.int32, (tok, 2 * hd), 1) < hd
        outs = []
        for pair in range(heads // 2):
            top = acc[pair, :tok, :]
            bot = acc[pair, tok:, :]
            num = jnp.where(half, top[:, : 2 * hd], bot[:, : 2 * hd])
            den = jnp.where(half, top[:, 2 * hd :], bot[:, 2 * hd :])
            outs.append(
                jnp.where(ok, num / jnp.where(ok, den, 1.0), 0.0).astype(jnp.bfloat16)
            )
        tend = dot(jnp.concatenate(outs, axis=1), wo_ref[...]).astype(jnp.bfloat16)
        out_ref[s] = tend
        if s == 0:
            gx1[0, 0] = (x.astype(jnp.float32) + tend.astype(jnp.float32)).astype(jnp.bfloat16)

    for chunk in range(4):
        for i, v in enumerate(verticals):

            @when(v[2])
            def _(i=i):
                vcopy(chunk, i).wait_send()

        for g in range(groups):
            for side in range(2):

                @when(sides[side][0], group_on[g])
                def _(g=g, side=side):
                    hcopy(chunk, g, side).wait_send()


def body(tiles, x, k, v, gain, w, wo, sharp, adj, marks, amount):
    tok, width = x.shape
    groups = 2 if tiles // TW == 2 else 3
    slots = 3 * groups
    vmem = pl.BlockSpec(memory_space=pltpu.VMEM)
    smem = pl.BlockSpec(memory_space=pltpu.SMEM)
    bf = jnp.bfloat16
    hd = width // sharp.shape[0]
    return pl.pallas_call(
        functools.partial(kernel, tiles),
        out_shape=jax.ShapeDtypeStruct((STEPS, tok, width), bf),
        in_specs=[vmem] * 6 + [smem] * 4,
        out_specs=vmem,
        scratch_shapes=[
            pltpu.VMEM((groups, 3, tok + 16, width), bf),
            pltpu.VMEM((groups, 3, tok, width), bf),
            pltpu.VMEM((groups, 3, tok, width), bf),
            pltpu.VMEM((groups, 3, tok, width), bf),
            pltpu.VMEM((slots, 3 * tok, width), bf),
            pltpu.VMEM((slots, 3 * tok, width), bf),
            pltpu.VMEM((slots, 2 * tok, 2 * hd), bf),
            pltpu.VMEM((width // (4 * hd), 4 * tok, 4 * hd), bf),
            pltpu.VMEM((width // (2 * hd), 2 * tok, 4 * hd), jnp.float32),
            pltpu.VMEM((4 * hd, 4 * hd), bf),
            pltpu.SemaphoreType.DMA((4, 3)),
            pltpu.SemaphoreType.DMA((4, 3)),
            pltpu.SemaphoreType.DMA((4, 3, 2)),
            pltpu.SemaphoreType.DMA((4, 3, 2)),
        ],
        compiler_params=pltpu.CompilerParams(
            collective_id=0, has_side_effects=True, vmem_limit_bytes=48 * 1024 * 1024
        ),
    )(x, k, v, gain.reshape(1, width), w, wo, sharp, adj, marks, amount)


def solution(mesh):
    part = ("grp", "tile")
    in_specs = (
        P(part, None),
        P(None, part, None),
        P(None, part, None),
        P(),
        P(),
        P(),
        P(),
        P(part, None),
        P(part),
        P(part),
    )
    return jax.shard_map(
        functools.partial(body, mesh.shape["tile"]),
        mesh=mesh,
        in_specs=in_specs,
        out_specs=P(None, part, None),
        check_vma=False,
    )
```

time: 404 us -> 56.6 us (0.14)
  the two profiles are of different devices: /device:TPU:27 before, /device:TPU:24 now
where the time goes in v1:
time: 56.6 us; the launch traced here: 56.3 us
  Pallas kernels  47.1 us (83%)
  local copies, waits for them, and re-layouts  8.5 us (15%)
  between operations  0.68 us (1%)
    pallas_call x1, Pallas kernels, body(): pl.pallas_call(functools.partial(kernel, tiles), out_shape=jax.ShapeDtype...  47.1 us
    unnamed x19, local copies, waits for them, and re-layouts  8.5 us

profile of v1, /device:TPU:24, one launch (start us, length us, event | category | flops | bytes accessed | tf_op | source)
XLA Modules:
  0.0 56.3 jit_solution(10362666601885835853)
XLA Ops:
  0.7 0.0 copy-start
  0.7 1.4 %copy-done = bf16[512,1536]{1,0:T(8,128)(2,1)S(1)} copy-done((bf16[512,1536]{1,0:T(8,128)(2,1)S(1)}, bf16[512,1536]{1,0:T(8,128)(2,1)}, u32[]{:S(2)}) %copy-start) | copy-done | bytes 1572888
  2.1 0.0 copy-start.1
  2.1 1.0 %copy-done.1 = bf16[512,512]{1,0:T(8,128)(2,1)S(1)} copy-done((bf16[512,512]{1,0:T(8,128)(2,1)S(1)}, bf16[512,512]{1,0:T(8,128)(2,1)}, u32[]{:S(2)}) %copy-start.1) | copy-done | bytes 524312
  3.1 0.0 copy-start.2
  3.1 0.9 %copy-done.2 = bf16[128,512]{1,0:T(8,128)(2,1)S(1)} copy-done((bf16[128,512]{1,0:T(8,128)(2,1)S(1)}, bf16[128,512]{1,0:T(8,128)(2,1)}, u32[]{:S(2)}) %copy-start.2) | copy-done | bytes 131096
  4.0 0.0 copy-start.3
  4.0 0.9 %copy-done.3 = bf16[1,128,512]{2,1,0:T(8,128)(2,1)S(1)} copy-done((bf16[1,128,512]{2,1,0:T(8,128)(2,1)S(1)}, bf16[1,128,512]{2,1,0:T(8,128)(2,1)}, u32[]{:S(2)}) %copy-start.3) | copy-done | bytes 131096
  4.9 0.0 copy-start.4
  4.9 0.9 %copy-done.4 = bf16[1,128,512]{2,1,0:T(8,128)(2,1)S(1)} copy-done((bf16[1,128,512]{2,1,0:T(8,128)(2,1)S(1)}, bf16[1,128,512]{2,1,0:T(8,128)(2,1)}, u32[]{:S(2)}) %copy-start.4) | copy-done | bytes 131096
  5.8 0.0 copy-start.5
  5.8 0.7 %copy-done.5 = f32[512]{0:T(512)S(1)} copy-done((f32[512]{0:T(512)S(1)}, f32[512]{0:T(512)}, u32[]{:S(2)}) %copy-start.5) | copy-done | bytes 2072
  6.5 0.0 copy-start.6
  6.5 0.7 %copy-done.6 = f32[8]{0:T(128)S(1)} copy-done((f32[8]{0:T(128)S(1)}, f32[8]{0:T(128)}, u32[]{:S(2)}) %copy-start.6) | copy-done | bytes 56
  7.2 0.0 copy-start.7
  7.2 0.7 %copy-done.7 = s32[1,8]{1,0:T(1,128)S(1)} copy-done((s32[1,8]{1,0:T(1,128)S(1)}, s32[1,8]{1,0:T(1,128)}, u32[]{:S(2)}) %copy-start.7) | copy-done | bytes 56
  7.8 0.0 copy-start.8
  7.8 0.7 %copy-done.8 = s32[8]{0:T(128)S(1)} copy-done((s32[8]{0:T(128)S(1)}, s32[8]{0:T(128)}, u32[]{:S(2)}) %copy-start.8) | copy-done | bytes 56
  8.5 47.1 %shard_map.100 = bf16[2,128,512]{2,1,0:T(8,128)(2,1)S(1)} custom-call(bf16[128,512]{1,0:T(8,128)(2,1)S(1)} %copy-done.2, bf16[1,128,512]{2,1,0:T(8,128)(2,1)S(1)} %copy-done.3, bf16[1,128,512]{2,1,0:T(8,128)(2,1)S(1)} %copy-done.4, f32[1,512]{1,0:T(1,128)S(1)} %bitcast.1, bf16[512,1536]{1,0:T(8,128)(2,1)S(1)} %copy-done, bf16[512,512]{1,0:T(8,128)(2,1)S(1)} %copy-done.1, ...), custom_call_target="tpu_custom_call" | custom-call | tf_op jit(solution)/shard_map/pallas_call | solution.py:341
  55.5 0.7 %copy.13 = bf16[2,128,512]{2,1,0:T(8,128)(2,1)} copy(bf16[2,128,512]{2,1,0:T(8,128)(2,1)S(1)} %shard_map.100) | data formatting | bytes 524288
Async XLA Ops:
  0.7 1.4 %copy-start = (bf16[512,1536]{1,0:T(8,128)(2,1)S(1)}, bf16[512,1536]{1,0:T(8,128)(2,1)}, u32[]{:S(2)}) copy-start(bf16[512,1536]{1,0:T(8,128)(2,1)} %w_ref.1) | copy-start | bytes 4718596
  2.1 1.0 %copy-start.1 = (bf16[512,512]{1,0:T(8,128)(2,1)S(1)}, bf16[512,512]{1,0:T(8,128)(2,1)}, u32[]{:S(2)}) copy-start(bf16[512,512]{1,0:T(8,128)(2,1)} %wo_ref.1) | copy-start | bytes 1572868
  3.1 0.9 %copy-start.2 = (bf16[128,512]{1,0:T(8,128)(2,1)S(1)}, bf16[128,512]{1,0:T(8,128)(2,1)}, u32[]{:S(2)}) copy-start(bf16[128,512]{1,0:T(8,128)(2,1)} %x_ref.1) | copy-start | bytes 393220
  4.0 0.9 %copy-start.3 = (bf16[1,128,512]{2,1,0:T(8,128)(2,1)S(1)}, bf16[1,128,512]{2,1,0:T(8,128)(2,1)}, u32[]{:S(2)}) copy-start(bf16[1,128,512]{2,1,0:T(8,128)(2,1)} %k_ref.1) | copy-start | bytes 393220
  4.9 0.9 %copy-start.4 = (bf16[1,128,512]{2,1,0:T(8,128)(2,1)S(1)}, bf16[1,128,512]{2,1,0:T(8,128)(2,1)}, u32[]{:S(2)}) copy-start(bf16[1,128,512]{2,1,0:T(8,128)(2,1)} %v_ref.1) | copy-start | bytes 393220
  5.8 0.7 %copy-start.5 = (f32[512]{0:T(512)S(1)}, f32[512]{0:T(512)}, u32[]{:S(2)}) copy-start(f32[512]{0:T(512)} %param.13) | copy-start | bytes 6148
  6.5 0.7 %copy-start.6 = (f32[8]{0:T(128)S(1)}, f32[8]{0:T(128)}, u32[]{:S(2)}) copy-start(f32[8]{0:T(128)} %sharp_ref.1) | copy-start | bytes 100
  7.2 0.7 %copy-start.7 = (s32[1,8]{1,0:T(1,128)S(1)}, s32[1,8]{1,0:T(1,128)}, u32[]{:S(2)}) copy-start(s32[1,8]{1,0:T(1,128)} %adj_ref.1) | copy-start | bytes 100
  7.8 0.7 %copy-start.8 = (s32[8]{0:T(128)S(1)}, s32[8]{0:T(128)}, u32[]{:S(2)}) copy-start(s32[8]{0:T(128)} %marks_ref.1) | copy-start | bytes 100

commit v2 on v1

v2 whole, which is shorter than its diff:
```python
import functools

import jax
import jax.numpy as jnp
from jax import lax
from jax.experimental import pallas as pl
from jax.experimental.pallas import tpu as pltpu
from jax.sharding import PartitionSpec as P

TW = 8
STEPS = 2
COLS = (0, -1, 1)
LOG2E = 1.4426950408889634
NT = (((1,), (1,)), ((), ()))
DIRECTIONS = ((-1, -1), (-1, 0), (-1, 1), (0, -1), (0, 1), (1, -1), (1, 0), (1, 1))


def dot(a, b):
    return jnp.dot(a, b, preferred_element_type=jnp.float32)


def kernel(
    tiles,
    x_hbm,
    k_hbm,
    v_hbm,
    gain_hbm,
    w_hbm,
    wo_hbm,
    sharp_hbm,
    adj_hbm,
    marks_hbm,
    amount_hbm,
    out_ref,
    k_ref,
    gain_ref,
    w_ref,
    wo_ref,
    sharp_ref,
    adj_ref,
    marks_ref,
    amount_ref,
    local,
    gx,
    gk,
    gv,
    ks,
    vs,
    ms,
    qs,
    nums,
    dens,
    psend,
    precv,
    ones_s,
    send_v,
    recv_v,
    send_h,
    recv_h,
    send_p,
    recv_p,
):
    tok, width = x_hbm.shape
    heads = sharp_hbm.shape[0]
    hd = width // heads
    qw = 4 * hd
    quads = width // qw
    rows = tiles // TW
    t = lax.axis_index("tile")
    row = t // TW
    col = t % TW
    two = rows == 2
    has_left = col > 0
    has_right = col < TW - 1
    if two:
        verticals = [(0, 0, None, jnp.where(row == 0, t + TW, t - TW))]
    else:
        verticals = [
            (0, 1, row > 0, jnp.maximum(t - TW, 0)),
            (1, 0, row < rows - 1, jnp.minimum(t + TW, tiles - 1)),
        ]
    sides = [
        (has_right, jnp.minimum(t + 1, tiles - 1), has_left),
        (has_left, jnp.maximum(t - 1, 0), has_right),
    ]

    def when(cond):
        return (lambda f: f()) if cond is None else pl.when(cond)

    def place(chunk, slot):
        if chunk == 0:
            return gx.at[0, slot]
        if chunk == 3:
            return gx.at[1, slot, :tok]
        return (gk if chunk == 1 else gv).at[slot]

    def remote(src, dst, send, recv, dev):
        return pltpu.make_async_remote_copy(
            src_ref=src,
            dst_ref=dst,
            send_sem=send,
            recv_sem=recv,
            device_id={"tile": dev},
            device_id_type=pl.DeviceIdType.MESH,
        )

    def vcopy(chunk, at, dev):
        c = chunk // 3
        return remote(
            place(chunk, 0), place(chunk, 3 + at), send_v.at[c, at], recv_v.at[c, at], dev
        )

    def hcopy(chunk, side):
        return remote(
            place(chunk, 0),
            place(chunk, 1 + side),
            send_h.at[chunk, side],
            recv_h.at[chunk, side],
            sides[side][1],
        )

    def pcopy(s, src, dst, q, dev):
        return remote(
            psend.at[s, src, q],
            precv.at[s, dst, q],
            send_p.at[s, dst, q],
            recv_p.at[s, dst, q],
            dev,
        )

    barrier = pltpu.get_barrier_semaphore()
    reach = [(v[2], v[3]) for v in verticals] + [(s[0], s[1]) for s in sides]
    for on, dev in reach:

        @when(on)
        def _(dev=dev):
            pl.semaphore_signal(
                barrier, inc=1, device_id={"tile": dev}, device_id_type=pl.DeviceIdType.MESH
            )

    loads = [
        (marks_hbm, marks_ref),
        (amount_hbm, amount_ref),
        (adj_hbm, adj_ref),
        (x_hbm, gx.at[0, 0, :tok]),
        (v_hbm.at[0], gv.at[0]),
        (k_hbm, k_ref),
        (gain_hbm, gain_ref),
        (w_hbm, w_ref),
        (sharp_hbm, sharp_ref),
        (wo_hbm, wo_ref),
    ]
    loads = [pltpu.make_async_copy(a, b, local.at[i]) for i, (a, b) in enumerate(loads)]
    for load in loads:
        load.start()
    blocks = marks_ref.shape[0]
    per = tok // blocks

    def validity(pos):
        m = jnp.zeros(pos.shape, jnp.int32)
        for b in range(blocks):
            m = jnp.where((pos >= b * per) & (pos < (b + 1) * per), marks_ref[b], m)
        return (m == 1) & (pos < amount_ref[0])

    ri = lax.broadcasted_iota(jnp.int32, (tok, tok), 0)
    ci = lax.broadcasted_iota(jnp.int32, (tok, tok), 1)
    loads[0].wait()
    loads[1].wait()
    loads[2].wait()
    ok = validity(ri)
    up8 = lax.broadcasted_iota(jnp.int32, (16, tok), 0) < 8
    for c, dc in enumerate(COLS):
        up = adj_ref[0, DIRECTIONS.index((-1, dc))]
        down = adj_ref[0, DIRECTIONS.index((1, dc))]
        gx[0, 0, tok:, (c + 1) * tok : (c + 2) * tok] = jnp.where(
            jnp.where(up8, up, down) == 1, 1.0, 0.0
        ).astype(jnp.bfloat16)
    gx[0, 0, tok:, :tok] = jnp.where(
        validity(lax.broadcasted_iota(jnp.int32, (16, tok), 1)), 1.0, 0.0
    ).astype(jnp.bfloat16)
    e0 = lax.broadcasted_iota(jnp.int32, (qw, qw), 0) >> 6
    e1 = lax.broadcasted_iota(jnp.int32, (qw, qw), 1) >> 6
    ones_s[...] = jnp.where(e0 == e1, 1.0 / hd, 0.0).astype(jnp.bfloat16)

    peers = 0
    for on, dev in reach:
        peers = peers + (1 if on is None else on.astype(jnp.int32))
    pl.semaphore_wait(barrier, peers)

    def start_vertical(chunk):
        for _, there, on, dev in verticals:

            @when(on)
            def _(there=there, dev=dev):
                vcopy(chunk, there, dev).start()

    def start_sides(chunk):
        for side in range(2):

            @when(sides[side][0])
            def _(side=side):
                hcopy(chunk, side).start()

    def unit(u):
        f = u.astype(jnp.float32)
        sq = (f * f).astype(jnp.bfloat16)
        mean = jnp.concatenate(
            [dot(sq[:, i : i + qw], ones_s[...]) for i in range(0, width, qw)], axis=1
        )
        return f * lax.rsqrt(mean + 1e-06)

    loads[3].wait()
    start_vertical(0)
    start_sides(0)
    loads[4].wait()
    start_sides(2)
    loads[5].wait()
    gk[0] = unit(k_ref[0]).astype(jnp.bfloat16)
    start_sides(1)

    for load in loads[6:]:
        load.wait()
    lane = lax.broadcasted_iota(jnp.int32, (1, width), 1)
    scale = jnp.zeros((1, width), jnp.float32)
    for h in range(heads):
        scale = jnp.where(
            (lane >= h * hd) & (lane < (h + 1) * hd), sharp_ref[h] * (LOG2E / hd), scale
        )
    hrow = lax.broadcasted_iota(jnp.int32, (16, qw), 0)
    hlane = lax.broadcasted_iota(jnp.int32, (16, qw), 1)
    pick = jnp.where(hlane == hrow * hd, 1.0, 0.0).astype(jnp.bfloat16)
    spread = jnp.where(
        (hlane >= hrow * hd) & (hlane < (hrow + 1) * hd), 1.0, 0.0
    ).astype(jnp.bfloat16)
    half = lax.broadcasted_iota(jnp.int32, (tok, 2 * hd), 1) < hd

    for side in range(2):

        @pl.when(jnp.logical_not(sides[side][2]))
        def _(n=1 + side):
            ks[n] = jnp.zeros(ks.shape[1:], jnp.bfloat16)
            vs[n] = jnp.zeros(vs.shape[1:], jnp.bfloat16)
            ms[n] = jnp.zeros(ms.shape[1:], jnp.bfloat16)

    def norm(x):
        f = x.astype(jnp.float32)
        r = lax.rsqrt(jnp.mean(f * f, axis=-1, keepdims=True) + 1e-06)
        return (f * r * gain_ref[...]).astype(jnp.bfloat16)

    def make_query(i, x):
        u = dot(norm(x), w_ref[:, :width]).astype(jnp.bfloat16)
        query = unit(u) * scale
        for q in range(quads):
            part = query[:, q * qw : (q + 1) * qw]
            lanes = lax.broadcasted_iota(jnp.int32, (tok, qw), 1)
            for a in range(4):
                qs[i, q, a * tok : (a + 1) * tok, :] = jnp.where(
                    (lanes >= a * hd) & (lanes < (a + 1) * hd), part, 0.0
                ).astype(jnp.bfloat16)

    def prepare(n):
        line = gx[0, n, tok:, :tok].astype(jnp.float32)[:1]
        m = jnp.sum(jnp.where(ri == ci, line, 0.0), axis=1, keepdims=True)
        mb = jnp.broadcast_to(m, (tok, 2 * hd)).astype(jnp.bfloat16)
        ms[n, :tok, :] = mb
        ms[n, tok:, :] = mb
        ks[n, :tok, :] = gk[n]
        vs[n, :tok, :] = (gv[n].astype(jnp.float32) * m).astype(jnp.bfloat16)

    def project(s, n):
        kv = dot(norm(gx[s, n, :tok, :]), w_ref[:, width:]).astype(jnp.bfloat16)
        base = (s + 1) * tok
        ks[n, base : base + tok, :] = unit(kv[:, :width]).astype(jnp.bfloat16)
        m = ms[n, :tok, :1].astype(jnp.float32)
        vs[n, base : base + tok, :] = (kv[:, width:].astype(jnp.float32) * m).astype(
            jnp.bfloat16
        )

    def attend(s, i, q, seen):
        sums = [None, None]
        for c in range(3):
            keys = ks[c, s * tok : (s + 2) * tok, q * qw : (q + 1) * qw]
            scores = lax.dot_general(qs[i, q], keys, NT, preferred_element_type=jnp.float32)
            p = jnp.exp2(scores).astype(jnp.bfloat16)
            for a in range(2):
                lo = (q * 2 + a) * 2 * hd
                vals = vs[c, s * tok : (s + 2) * tok, lo : lo + 2 * hd]
                r = dot(p[a * 2 * tok : (a + 1) * 2 * tok], jnp.concatenate([vals, ms[c]], axis=1))
                if seen[c] is not None:
                    r = r * seen[c]
                sums[a] = r if sums[a] is None else sums[a] + r
        num, den = [], []
        for r in sums:
            top, bot = r[:tok], r[tok:]
            num.append(jnp.where(half, top[:, : 2 * hd], bot[:, : 2 * hd]))
            den.append(jnp.where(half, top[:, 2 * hd :], bot[:, 2 * hd :]))
        return jnp.concatenate(num, axis=1), jnp.concatenate(den, axis=1)

    own_seen = [None]
    for dc in (-1, 1):
        own_seen.append(jnp.where(adj_ref[0, DIRECTIONS.index((0, dc))] == 1, 1.0, 0.0))

    for s in range(STEPS):
        if s > 0:
            start_vertical(3)
            start_sides(3)
        make_query(0, gx[s, 0, :tok, :])
        if s == 0:
            prepare(0)
        project(s, 0)
        for here, _, on, dev in verticals:

            @when(on)
            def _(here=here, dev=dev):
                vcopy(3 * s, here, dev).wait_recv()
                make_query(1 + here, gx[s, 3 + here, :tok, :])

        for side in range(2):

            @pl.when(sides[side][2])
            def _(side=side):
                for chunk in (0, 2, 1) if s == 0 else (3,):
                    hcopy(chunk, side).wait_recv()
                if s == 0:
                    prepare(1 + side)
                project(s, 1 + side)

        for here, there, on, dev in verticals:

            @when(on)
            def _(here=here, there=there, dev=dev):
                lines = gx[0, 3 + here, tok:, :].astype(jnp.float32)
                up, down = lines[:1], lines[8:9]
                if two:
                    line = jnp.where(row == 0, up, down)
                else:
                    line = down if here == 0 else up
                seen = []
                for c, dc in enumerate(COLS):
                    part = line[:, (c + 1) * tok : (c + 2) * tok]
                    seen.append(jnp.concatenate([part] * (qw // tok), axis=1))
                for q in range(quads):
                    num, den = attend(s, 1 + here, q, seen)
                    psend[s, here, q, :tok, :] = num.astype(jnp.bfloat16)
                    low = lax.dot_general(
                        pick, den.astype(jnp.bfloat16), NT, preferred_element_type=jnp.float32
                    ).astype(jnp.bfloat16)
                    psend[s, here, q, tok:, :] = jnp.concatenate([low] * (qw // tok), axis=1)
                    pcopy(s, here, there, q, dev).start()

        for q in range(quads):
            nums[q], dens[q] = attend(s, 0, q, own_seen)
        for here, _, on, dev in verticals:
            for q in range(quads):

                @when(on)
                def _(here=here, dev=dev, q=q):
                    pcopy(s, here, here, q, dev).wait_recv()
                    nums[q] += precv[s, here, q, :tok, :].astype(jnp.float32)
                    dens[q] += lax.dot_general(
                        precv[s, here, q, tok:, :tok],
                        spread,
                        (((0,), (0,)), ((), ())),
                        preferred_element_type=jnp.float32,
                    )

        valid = jnp.concatenate([ok] * (qw // tok), axis=1)
        outs = [
            jnp.where(valid, nums[q] / jnp.where(valid, dens[q], 1.0), 0.0).astype(jnp.bfloat16)
            for q in range(quads)
        ]
        tend = dot(jnp.concatenate(outs, axis=1), wo_ref[...]).astype(jnp.bfloat16)
        if s == 0:
            x = gx[0, 0, :tok, :].astype(jnp.float32)
            gx[1, 0, :tok, :] = (x + tend.astype(jnp.float32)).astype(jnp.bfloat16)
        out_ref[s] = tend

    for here, there, on, dev in verticals:

        @when(on)
        def _(here=here, there=there, dev=dev):
            for s in range(STEPS):
                vcopy(3 * s, there, dev).wait_send()
                for q in range(quads):
                    pcopy(s, here, there, q, dev).wait_send()

    for side in range(2):

        @pl.when(sides[side][0])
        def _(side=side):
            for chunk in range(4):
                hcopy(chunk, side).wait_send()


def body(tiles, x, k, v, gain, w, wo, sharp, adj, marks, amount):
    tok, width = x.shape
    nv = 1 if tiles // TW == 2 else 2
    vmem = pl.BlockSpec(memory_space=pltpu.VMEM)
    hbm = pl.BlockSpec(memory_space=pltpu.HBM)
    bf = jnp.bfloat16
    hd = width // sharp.shape[0]
    qw = 4 * hd
    quads = width // qw
    return pl.pallas_call(
        functools.partial(kernel, tiles),
        out_shape=jax.ShapeDtypeStruct((STEPS, tok, width), bf),
        in_specs=[hbm] * 10,
        out_specs=vmem,
        scratch_shapes=[
            pltpu.VMEM(k.shape, bf),
            pltpu.VMEM((1, width), jnp.float32),
            pltpu.VMEM(w.shape, bf),
            pltpu.VMEM(wo.shape, bf),
            pltpu.SMEM(sharp.shape, jnp.float32),
            pltpu.SMEM(adj.shape, jnp.int32),
            pltpu.SMEM(marks.shape, jnp.int32),
            pltpu.SMEM(amount.shape, jnp.int32),
            pltpu.SemaphoreType.DMA((10,)),
            pltpu.VMEM((STEPS, 3 + nv, tok + 16, width), bf),
            pltpu.VMEM((3, tok, width), bf),
            pltpu.VMEM((3, tok, width), bf),
            pltpu.VMEM((3, 3 * tok, width), bf),
            pltpu.VMEM((3, 3 * tok, width), bf),
            pltpu.VMEM((3, 2 * tok, 2 * hd), bf),
            pltpu.VMEM((1 + nv, quads, 4 * tok, qw), bf),
            pltpu.VMEM((quads, tok, qw), jnp.float32),
            pltpu.VMEM((quads, tok, qw), jnp.float32),
            pltpu.VMEM((STEPS, nv, quads, tok + 16, qw), bf),
            pltpu.VMEM((STEPS, nv, quads, tok + 16, qw), bf),
            pltpu.VMEM((qw, qw), bf),
            pltpu.SemaphoreType.DMA((STEPS, nv)),
            pltpu.SemaphoreType.DMA((STEPS, nv)),
            pltpu.SemaphoreType.DMA((4, 2)),
            pltpu.SemaphoreType.DMA((4, 2)),
            pltpu.SemaphoreType.DMA((STEPS, nv, quads)),
            pltpu.SemaphoreType.DMA((STEPS, nv, quads)),
        ],
        compiler_params=pltpu.CompilerParams(
            collective_id=0, has_side_effects=True, vmem_limit_bytes=62 * 1024 * 1024
        ),
    )(x, k, v, gain.reshape(1, width), w, wo, sharp, adj, marks, amount)


def solution(mesh):
    part = ("grp", "tile")
    in_specs = (
        P(part, None),
        P(None, part, None),
        P(None, part, None),
        P(),
        P(),
        P(),
        P(),
        P(part, None),
        P(part),
        P(part),
    )
    return jax.shard_map(
        functools.partial(body, mesh.shape["tile"]),
        mesh=mesh,
        in_specs=in_specs,
        out_specs=P(None, part, None),
        check_vma=False,
    )
```

time: 56.6 us -> 42.9 us (0.76)
  the two profiles are of different devices: /device:TPU:24 before, /device:TPU:5 now
where the time goes in v2:
time: 42.9 us; the launch traced here: 42.1 us
  Pallas kernels  39.8 us (93%)
  local copies, waits for them, and re-layouts  1.67 us (4%)
  between operations  0.66 us (2%)
    pallas_call x1, Pallas kernels, body(): pl.pallas_call(functools.partial(kernel, tiles), out_shape=jax.ShapeDtype...  39.8 us
    unnamed x1, local copies, waits for them, and re-layouts  1.67 us

profile of v2, /device:TPU:5, one launch (start us, length us, event | category | flops | bytes accessed | tf_op | source)
XLA Modules:
  0.0 42.1 jit_solution(16956929828838803231)
XLA Ops:
  0.7 39.8 %shard_map.100 = bf16[2,128,512]{2,1,0:T(8,128)(2,1)} custom-call(bf16[128,512]{1,0:T(8,128)(2,1)} %x_hbm.1, bf16[1,128,512]{2,1,0:T(8,128)(2,1)} %k_hbm.1, bf16[1,128,512]{2,1,0:T(8,128)(2,1)} %v_hbm.1, f32[1,512]{1,0:T(1,128)} %bitcast.1, bf16[512,1536]{1,0:T(8,128)(2,1)} %w_hbm.1, bf16[512,512]{1,0:T(8,128)(2,1)} %wo_hbm.1, f32[8]{0:T(128)} %sharp_hbm.1, ...), custom_call_target="tpu_custom_call" | custom-call | tf_op jit(solution)/shard_map/pallas_call | solution.py:404
  40.4 1.7 %copy.13 = bf16[2,128,512]{2,1,0:T(8,128)(2,1)} copy(bf16[2,128,512]{2,1,0:T(8,128)(2,1)} %shard_map.100) | data formatting | bytes 524288

commit v3 on v2

v3 whole, which is shorter than its diff:
```python
import functools

import jax
import jax.numpy as jnp
from jax import lax
from jax.experimental import pallas as pl
from jax.experimental.pallas import tpu as pltpu
from jax.sharding import PartitionSpec as P

TW = 8
STEPS = 2
COLS = (0, -1, 1)
LOG2E = 1.4426950408889634
NT = (((1,), (1,)), ((), ()))
DIRECTIONS = ((-1, -1), (-1, 0), (-1, 1), (0, -1), (0, 1), (1, -1), (1, 0), (1, 1))


def dot(a, b):
    return jnp.dot(a, b, preferred_element_type=jnp.float32)


def kernel(
    tiles,
    x_hbm,
    k_hbm,
    v_hbm,
    gain_hbm,
    w_hbm,
    wo_hbm,
    sharp_hbm,
    adj_hbm,
    marks_hbm,
    amount_hbm,
    out_ref,
    k_ref,
    gain_ref,
    w_ref,
    wo_ref,
    sharp_ref,
    adj_ref,
    marks_ref,
    amount_ref,
    local,
    gx,
    gk,
    gv,
    ks,
    vs,
    ms,
    qs,
    nums,
    dens,
    psend,
    precv,
    lsend,
    lrecv,
    ones_s,
    send_v,
    recv_v,
    send_h,
    recv_h,
    send_p,
    recv_p,
):
    tok, width = x_hbm.shape
    heads = sharp_hbm.shape[0]
    hd = width // heads
    qw = 4 * hd
    quads = width // qw
    ht = tok // 2
    base = 16
    rows = tiles // TW
    t = lax.axis_index("tile")
    row = t // TW
    col = t % TW
    two = rows == 2
    has_left = col > 0
    has_right = col < TW - 1
    if two:
        verticals = [(0, 0, None, jnp.where(row == 0, t + TW, t - TW))]
    else:
        verticals = [
            (0, 1, row > 0, jnp.maximum(t - TW, 0)),
            (1, 0, row < rows - 1, jnp.minimum(t + TW, tiles - 1)),
        ]
    sides = [
        (has_right, jnp.minimum(t + 1, tiles - 1), has_left),
        (has_left, jnp.maximum(t - 1, 0), has_right),
    ]

    def when(cond):
        return (lambda f: f()) if cond is None else pl.when(cond)

    def place(chunk, slot):
        if chunk == 0:
            return gx.at[0, slot]
        if chunk >= 3:
            lo = base + (chunk - 3) * ht
            return gx.at[1, slot, lo : lo + ht]
        return (gk if chunk == 1 else gv).at[slot]

    def remote(src, dst, send, recv, dev):
        return pltpu.make_async_remote_copy(
            src_ref=src,
            dst_ref=dst,
            send_sem=send,
            recv_sem=recv,
            device_id={"tile": dev},
            device_id_type=pl.DeviceIdType.MESH,
        )

    def vcopy(s, h, at, dev):
        lo = 0 if s == 0 and h == 0 else base + h * ht
        hi = base + (h + 1) * ht
        return remote(
            gx.at[s, 0, lo:hi],
            gx.at[s, 3 + at, lo:hi],
            send_v.at[s, h, at],
            recv_v.at[s, h, at],
            dev,
        )

    def hcopy(chunk, side):
        return remote(
            place(chunk, 0),
            place(chunk, 1 + side),
            send_h.at[chunk, side],
            recv_h.at[chunk, side],
            sides[side][1],
        )

    def pcopies(s, src, dst, h, dev):
        return [
            remote(a.at[s, src, h], b.at[s, dst, h], send_p.at[s, dst, k], recv_p.at[s, dst, k], dev)
            for k, a, b in ((2 * h, lsend, lrecv), (2 * h + 1, psend, precv))
        ]

    barrier = pltpu.get_barrier_semaphore()
    reach = [(v[2], v[3]) for v in verticals] + [(s[0], s[1]) for s in sides]
    for on, dev in reach:

        @when(on)
        def _(dev=dev):
            pl.semaphore_signal(
                barrier, inc=1, device_id={"tile": dev}, device_id_type=pl.DeviceIdType.MESH
            )

    loads = [
        (marks_hbm, marks_ref),
        (amount_hbm, amount_ref),
        (adj_hbm, adj_ref),
        (x_hbm, gx.at[0, 0, base:]),
        (v_hbm.at[0], gv.at[0]),
        (k_hbm, k_ref),
        (gain_hbm, gain_ref),
        (w_hbm, w_ref),
        (sharp_hbm, sharp_ref),
        (wo_hbm, wo_ref),
    ]
    loads = [pltpu.make_async_copy(a, b, local.at[i]) for i, (a, b) in enumerate(loads)]
    for load in loads:
        load.start()
    blocks = marks_ref.shape[0]
    per = tok // blocks

    def validity(pos):
        m = jnp.zeros(pos.shape, jnp.int32)
        for b in range(blocks):
            m = jnp.where((pos >= b * per) & (pos < (b + 1) * per), marks_ref[b], m)
        return (m == 1) & (pos < amount_ref[0])

    ri = lax.broadcasted_iota(jnp.int32, (tok, tok), 0)
    ci = lax.broadcasted_iota(jnp.int32, (tok, tok), 1)
    loads[0].wait()
    loads[1].wait()
    loads[2].wait()
    ok = validity(ri)
    up8 = lax.broadcasted_iota(jnp.int32, (16, tok), 0) < 8
    for c, dc in enumerate(COLS):
        up = adj_ref[0, DIRECTIONS.index((-1, dc))]
        down = adj_ref[0, DIRECTIONS.index((1, dc))]
        gx[0, 0, :base, (c + 1) * tok : (c + 2) * tok] = jnp.where(
            jnp.where(up8, up, down) == 1, 1.0, 0.0
        ).astype(jnp.bfloat16)
    gx[0, 0, :base, :tok] = jnp.where(
        validity(lax.broadcasted_iota(jnp.int32, (16, tok), 1)), 1.0, 0.0
    ).astype(jnp.bfloat16)
    e0 = lax.broadcasted_iota(jnp.int32, (qw, qw), 0) >> 6
    e1 = lax.broadcasted_iota(jnp.int32, (qw, qw), 1) >> 6
    ones_s[...] = jnp.where(e0 == e1, 1.0 / hd, 0.0).astype(jnp.bfloat16)

    peers = 0
    for on, dev in reach:
        peers = peers + (1 if on is None else on.astype(jnp.int32))
    pl.semaphore_wait(barrier, peers)

    def start_vertical(s, h):
        for _, there, on, dev in verticals:

            @when(on)
            def _(there=there, dev=dev):
                vcopy(s, h, there, dev).start()

    def start_sides(chunk):
        for side in range(2):

            @when(sides[side][0])
            def _(side=side):
                hcopy(chunk, side).start()

    def unit(u):
        f = u.astype(jnp.float32)
        sq = (f * f).astype(jnp.bfloat16)
        mean = jnp.concatenate(
            [dot(sq[:, i : i + qw], ones_s[...]) for i in range(0, width, qw)], axis=1
        )
        return f * lax.rsqrt(mean + 1e-06)

    loads[3].wait()
    start_vertical(0, 0)
    start_sides(0)
    loads[4].wait()
    start_sides(2)
    loads[5].wait()
    gk[0] = unit(k_ref[0]).astype(jnp.bfloat16)
    start_sides(1)

    for load in loads[6:]:
        load.wait()
    lane = lax.broadcasted_iota(jnp.int32, (1, width), 1)
    scale = jnp.zeros((1, width), jnp.float32)
    for h in range(heads):
        scale = jnp.where(
            (lane >= h * hd) & (lane < (h + 1) * hd), sharp_ref[h] * (LOG2E / hd), scale
        )
    hrow = lax.broadcasted_iota(jnp.int32, (16, width), 0)
    hlane = lax.broadcasted_iota(jnp.int32, (16, width), 1)
    pick = jnp.where(hlane == hrow * hd, 1.0, 0.0).astype(jnp.bfloat16)
    spread = jnp.where(
        (hlane >= hrow * hd) & (hlane < (hrow + 1) * hd), 1.0, 0.0
    ).astype(jnp.bfloat16)
    half = lax.broadcasted_iota(jnp.int32, (ht, 2 * hd), 1) < hd

    for side in range(2):

        @pl.when(jnp.logical_not(sides[side][2]))
        def _(n=1 + side):
            ks[n] = jnp.zeros(ks.shape[1:], jnp.bfloat16)
            vs[n] = jnp.zeros(vs.shape[1:], jnp.bfloat16)
            ms[n] = jnp.zeros(ms.shape[1:], jnp.bfloat16)

    def norm(x):
        f = x.astype(jnp.float32)
        r = lax.rsqrt(jnp.mean(f * f, axis=-1, keepdims=True) + 1e-06)
        return (f * r * gain_ref[...]).astype(jnp.bfloat16)

    lanes = lax.broadcasted_iota(jnp.int32, (ht, qw), 1)

    def make_query(i, h, x):
        u = dot(norm(x), w_ref[:, :width]).astype(jnp.bfloat16)
        query = unit(u) * scale
        for k in range(x.shape[0] // ht):
            for q in range(quads):
                part = query[k * ht : (k + 1) * ht, q * qw : (q + 1) * qw]
                for a in range(4):
                    qs[i, h + k, q, a * ht : (a + 1) * ht, :] = jnp.where(
                        (lanes >= a * hd) & (lanes < (a + 1) * hd), part, 0.0
                    ).astype(jnp.bfloat16)

    def prepare(n):
        line = gx[0, n, :base, :tok].astype(jnp.float32)[:1]
        m = jnp.sum(jnp.where(ri == ci, line, 0.0), axis=1, keepdims=True)
        mb = jnp.broadcast_to(m, (tok, 2 * hd)).astype(jnp.bfloat16)
        ms[n, :tok, :] = mb
        ms[n, tok:, :] = mb
        ks[n, :tok, :] = gk[n]
        vs[n, :tok, :] = (gv[n].astype(jnp.float32) * m).astype(jnp.bfloat16)

    def project(s, n):
        kv = dot(norm(gx[s, n, base:, :]), w_ref[:, width:]).astype(jnp.bfloat16)
        lo = (s + 1) * tok
        ks[n, lo : lo + tok, :] = unit(kv[:, :width]).astype(jnp.bfloat16)
        m = ms[n, :tok, :1].astype(jnp.float32)
        vs[n, lo : lo + tok, :] = (kv[:, width:].astype(jnp.float32) * m).astype(
            jnp.bfloat16
        )

    def attend(s, i, h, seen):
        parts = [attend_quad(s, i, h, q, seen) for q in range(quads)]
        return [jnp.concatenate([p[k] for p in parts], axis=1) for k in range(2)]

    def attend_quad(s, i, h, q, seen):
        sums = [None, None]
        for c in range(3):
            keys = ks[c, s * tok : (s + 2) * tok, q * qw : (q + 1) * qw]
            scores = lax.dot_general(qs[i, h, q], keys, NT, preferred_element_type=jnp.float32)
            p = jnp.exp2(scores).astype(jnp.bfloat16)
            for a in range(2):
                lo = (q * 2 + a) * 2 * hd
                vals = vs[c, s * tok : (s + 2) * tok, lo : lo + 2 * hd]
                r = dot(p[a * 2 * ht : (a + 1) * 2 * ht], jnp.concatenate([vals, ms[c]], axis=1))
                if seen[c] is not None:
                    r = r * seen[c]
                sums[a] = r if sums[a] is None else sums[a] + r
        num, den = [], []
        for r in sums:
            top, bot = r[:ht], r[ht:]
            num.append(jnp.where(half, top[:, : 2 * hd], bot[:, : 2 * hd]))
            den.append(jnp.where(half, top[:, 2 * hd :], bot[:, 2 * hd :]))
        return jnp.concatenate(num, axis=1), jnp.concatenate(den, axis=1)

    own_seen = [None]
    for dc in (-1, 1):
        own_seen.append(jnp.where(adj_ref[0, DIRECTIONS.index((0, dc))] == 1, 1.0, 0.0))

    for s in range(STEPS):
        make_query(0, 0, gx[s, 0, base:, :])
        if s == 0:
            for _, there, on, dev in verticals:

                @when(on)
                def _(there=there, dev=dev):
                    vcopy(0, 0, there, dev).wait_send()
                    vcopy(0, 1, there, dev).start()

            prepare(0)
        project(s, 0)
        for side in range(2):

            @pl.when(sides[side][2])
            def _(side=side):
                for chunk in (0, 2, 1) if s == 0 else (3, 4):
                    hcopy(chunk, side).wait_recv()
                if s == 0:
                    prepare(1 + side)
                project(s, 1 + side)

        for h in range(2):
            for here, there, on, dev in verticals:

                @when(on)
                def _(here=here, there=there, dev=dev):
                    vcopy(s, h, here, dev).wait_recv()
                    lo = base + h * ht
                    make_query(1 + here, h, gx[s, 3 + here, lo : lo + ht, :])
                    lines = gx[0, 3 + here, :base, :].astype(jnp.float32)
                    up, down = lines[:1], lines[8:9]
                    if two:
                        line = jnp.where(row == 0, up, down)
                    else:
                        line = down if here == 0 else up
                    seen = []
                    for c in range(3):
                        part = line[:, (c + 1) * tok : (c + 2) * tok]
                        seen.append(jnp.concatenate([part] * (qw // tok), axis=1))
                    num, den = attend(s, 1 + here, h, seen)
                    psend[s, here, h] = num.astype(jnp.bfloat16)
                    low = lax.dot_general(
                        pick, den.astype(jnp.bfloat16), NT, preferred_element_type=jnp.float32
                    ).astype(jnp.bfloat16)
                    lsend[s, here, h] = jnp.concatenate([low] * 2, axis=1)
                    for copy in pcopies(s, here, there, h, dev):
                        copy.start()

            nums[h], dens[h] = attend(s, 0, h, own_seen)

        for h in range(2):
            for here, _, on, dev in verticals:

                @when(on)
                def _(here=here, dev=dev):
                    for copy in pcopies(s, here, here, h, dev):
                        copy.wait_recv()
                    nums[h] += precv[s, here, h].astype(jnp.float32)
                    dens[h] += lax.dot_general(
                        lrecv[s, here, h],
                        spread,
                        (((0,), (0,)), ((), ())),
                        preferred_element_type=jnp.float32,
                    )[:ht]

            valid = jnp.concatenate([ok[h * ht : (h + 1) * ht]] * (width // tok), axis=1)
            att = jnp.where(valid, nums[h] / jnp.where(valid, dens[h], 1.0), 0.0)
            tend = dot(att.astype(jnp.bfloat16), wo_ref[...]).astype(jnp.bfloat16)
            if s == 0:
                lo = base + h * ht
                x = gx[0, 0, lo : lo + ht, :].astype(jnp.float32)
                gx[1, 0, lo : lo + ht, :] = (x + tend.astype(jnp.float32)).astype(jnp.bfloat16)
                start_vertical(1, h)
                start_sides(3 + h)
            out_ref[s, h * ht : (h + 1) * ht, :] = tend

    for here, there, on, dev in verticals:

        @when(on)
        def _(here=here, there=there, dev=dev):
            for s, h in ((0, 1), (1, 0), (1, 1)):
                vcopy(s, h, there, dev).wait_send()
            for s in range(STEPS):
                for h in range(2):
                    for copy in pcopies(s, here, there, h, dev):
                        copy.wait_send()

    for side in range(2):

        @pl.when(sides[side][0])
        def _(side=side):
            for chunk in range(5):
                hcopy(chunk, side).wait_send()


def body(tiles, x, k, v, gain, w, wo, sharp, adj, marks, amount):
    tok, width = x.shape
    nv = 1 if tiles // TW == 2 else 2
    vmem = pl.BlockSpec(memory_space=pltpu.VMEM)
    hbm = pl.BlockSpec(memory_space=pltpu.HBM)
    bf = jnp.bfloat16
    hd = width // sharp.shape[0]
    qw = 4 * hd
    quads = width // qw
    return pl.pallas_call(
        functools.partial(kernel, tiles),
        out_shape=jax.ShapeDtypeStruct((STEPS, tok, width), bf),
        in_specs=[hbm] * 10,
        out_specs=vmem,
        scratch_shapes=[
            pltpu.VMEM(k.shape, bf),
            pltpu.VMEM((1, width), jnp.float32),
            pltpu.VMEM(w.shape, bf),
            pltpu.VMEM(wo.shape, bf),
            pltpu.SMEM(sharp.shape, jnp.float32),
            pltpu.SMEM(adj.shape, jnp.int32),
            pltpu.SMEM(marks.shape, jnp.int32),
            pltpu.SMEM(amount.shape, jnp.int32),
            pltpu.SemaphoreType.DMA((10,)),
            pltpu.VMEM((STEPS, 3 + nv, tok + 16, width), bf),
            pltpu.VMEM((3, tok, width), bf),
            pltpu.VMEM((3, tok, width), bf),
            pltpu.VMEM((3, 3 * tok, width), bf),
            pltpu.VMEM((3, 3 * tok, width), bf),
            pltpu.VMEM((3, 2 * tok, 2 * hd), bf),
            pltpu.VMEM((1 + nv, 2, quads, 2 * tok, qw), bf),
            pltpu.VMEM((2, tok // 2, width), jnp.float32),
            pltpu.VMEM((2, tok // 2, width), jnp.float32),
            pltpu.VMEM((STEPS, nv, 2, tok // 2, width), bf),
            pltpu.VMEM((STEPS, nv, 2, tok // 2, width), bf),
            pltpu.VMEM((STEPS, nv, 2, 16, tok), bf),
            pltpu.VMEM((STEPS, nv, 2, 16, tok), bf),
            pltpu.VMEM((qw, qw), bf),
            pltpu.SemaphoreType.DMA((STEPS, 2, nv)),
            pltpu.SemaphoreType.DMA((STEPS, 2, nv)),
            pltpu.SemaphoreType.DMA((5, 2)),
            pltpu.SemaphoreType.DMA((5, 2)),
            pltpu.SemaphoreType.DMA((STEPS, nv, 4)),
            pltpu.SemaphoreType.DMA((STEPS, nv, 4)),
        ],
        compiler_params=pltpu.CompilerParams(
            collective_id=0, has_side_effects=True, vmem_limit_bytes=62 * 1024 * 1024
        ),
    )(x, k, v, gain.reshape(1, width), w, wo, sharp, adj, marks, amount)


def solution(mesh):
    part = ("grp", "tile")
    in_specs = (
        P(part, None),
        P(None, part, None),
        P(None, part, None),
        P(),
        P(),
        P(),
        P(),
        P(part, None),
        P(part),
        P(part),
    )
    return jax.shard_map(
        functools.partial(body, mesh.shape["tile"]),
        mesh=mesh,
        in_specs=in_specs,
        out_specs=P(None, part, None),
        check_vma=False,
    )
```

time: 42.9 us -> 40.4 us (0.942); the launches traced: 42.1 us -> 40.2 us
  Pallas kernels: 39.8 us -> 37.9 us
    pallas_call x1, Pallas kernels: 39.8 us -> 37.9 us  [body(): pl.pallas_call(functools.partial(kernel, tiles), out_shape=jax.ShapeDtype...]
where the time goes in v3:
time: 40.4 us; the launch traced here: 40.2 us
  Pallas kernels  37.9 us (94%)
  local copies, waits for them, and re-layouts  1.67 us (4%)
  between operations  0.66 us (2%)
    pallas_call x1, Pallas kernels, body(): pl.pallas_call(functools.partial(kernel, tiles), out_shape=jax.ShapeDtype...  37.9 us
    unnamed x1, local copies, waits for them, and re-layouts  1.67 us

profile of v3, /device:TPU:5, one launch (start us, length us, event | category | flops | bytes accessed | tf_op | source)
XLA Modules:
  0.0 40.2 jit_solution(3651832107659194505)
XLA Ops:
  0.7 37.9 %shard_map.100 = bf16[2,128,512]{2,1,0:T(8,128)(2,1)} custom-call(bf16[128,512]{1,0:T(8,128)(2,1)} %x_hbm.1, bf16[1,128,512]{2,1,0:T(8,128)(2,1)} %k_hbm.1, bf16[1,128,512]{2,1,0:T(8,128)(2,1)} %v_hbm.1, f32[1,512]{1,0:T(1,128)} %bitcast.1, bf16[512,1536]{1,0:T(8,128)(2,1)} %w_hbm.1, bf16[512,512]{1,0:T(8,128)(2,1)} %wo_hbm.1, f32[8]{0:T(128)} %sharp_hbm.1, ...), custom_call_target="tpu_custom_call" | custom-call | tf_op jit(solution)/shard_map/pallas_call | solution.py:421
  38.6 1.7 %copy.13 = bf16[2,128,512]{2,1,0:T(8,128)(2,1)} copy(bf16[2,128,512]{2,1,0:T(8,128)(2,1)} %shard_map.100) | data formatting | bytes 524288

commit v4 on v3

--- a/solution.py
+++ b/solution.py
@@ -32,7 +32,6 @@
     marks_hbm,
     amount_hbm,
     out_ref,
-    k_ref,
     gain_ref,
     w_ref,
     wo_ref,
@@ -151,7 +150,7 @@
         (adj_hbm, adj_ref),
         (x_hbm, gx.at[0, 0, base:]),
         (v_hbm.at[0], gv.at[0]),
-        (k_hbm, k_ref),
+        (k_hbm.at[0], gk.at[0]),
         (gain_hbm, gain_ref),
         (w_hbm, w_ref),
         (sharp_hbm, sharp_ref),
@@ -222,7 +221,6 @@
     loads[4].wait()
     start_sides(2)
     loads[5].wait()
-    gk[0] = unit(k_ref[0]).astype(jnp.bfloat16)
     start_sides(1)
 
     for load in loads[6:]:
@@ -273,7 +271,7 @@
         mb = jnp.broadcast_to(m, (tok, 2 * hd)).astype(jnp.bfloat16)
         ms[n, :tok, :] = mb
         ms[n, tok:, :] = mb
-        ks[n, :tok, :] = gk[n]
+        ks[n, :tok, :] = unit(gk[n]).astype(jnp.bfloat16)
         vs[n, :tok, :] = (gv[n].astype(jnp.float32) * m).astype(jnp.bfloat16)
 
     def project(s, n):
@@ -320,7 +318,6 @@
 
                 @when(on)
                 def _(there=there, dev=dev):
-                    vcopy(0, 0, there, dev).wait_send()
                     vcopy(0, 1, there, dev).start()
 
             prepare(0)
@@ -394,7 +391,7 @@
 
         @when(on)
         def _(here=here, there=there, dev=dev):
-            for s, h in ((0, 1), (1, 0), (1, 1)):
+            for s, h in ((0, 0), (0, 1), (1, 0), (1, 1)):
                 vcopy(s, h, there, dev).wait_send()
             for s in range(STEPS):
                 for h in range(2):
@@ -424,7 +421,6 @@
         in_specs=[hbm] * 10,
         out_specs=vmem,
         scratch_shapes=[
-            pltpu.VMEM(k.shape, bf),
             pltpu.VMEM((1, width), jnp.float32),
             pltpu.VMEM(w.shape, bf),
             pltpu.VMEM(wo.shape, bf),

time: 40.4 us -> 39.7 us (0.983)
  Pallas kernels: 37.9 us -> 37.2 us
    pallas_call x1, Pallas kernels: 37.9 us -> 37.2 us  [body(): pl.pallas_call(functools.partial(kernel, tiles), out_shape=jax.ShapeDtype...]
where the time goes in v4:
time: 39.7 us; the launch traced here: 39.5 us
  Pallas kernels  37.2 us (94%)
  local copies, waits for them, and re-layouts  1.67 us (4%)
  between operations  0.66 us (2%)
    pallas_call x1, Pallas kernels, body(): pl.pallas_call(functools.partial(kernel, tiles), out_shape=jax.ShapeDtype...  37.2 us
    unnamed x1, local copies, waits for them, and re-layouts  1.67 us

profile of v4, /device:TPU:5, one launch (start us, length us, event | category | flops | bytes accessed | tf_op | source)
XLA Modules:
  0.0 39.5 jit_solution(17578607195105766435)
XLA Ops:
  0.7 37.2 %shard_map.100 = bf16[2,128,512]{2,1,0:T(8,128)(2,1)} custom-call(bf16[128,512]{1,0:T(8,128)(2,1)} %x_hbm.1, bf16[1,128,512]{2,1,0:T(8,128)(2,1)} %k_hbm.1, bf16[1,128,512]{2,1,0:T(8,128)(2,1)} %v_hbm.1, f32[1,512]{1,0:T(1,128)} %bitcast.1, bf16[512,1536]{1,0:T(8,128)(2,1)} %w_hbm.1, bf16[512,512]{1,0:T(8,128)(2,1)} %wo_hbm.1, f32[8]{0:T(128)} %sharp_hbm.1, ...), custom_call_target="tpu_custom_call" | custom-call | tf_op jit(solution)/shard_map/pallas_call | solution.py:418
  37.8 1.7 %copy.13 = bf16[2,128,512]{2,1,0:T(8,128)(2,1)} copy(bf16[2,128,512]{2,1,0:T(8,128)(2,1)} %shard_map.100) | data formatting | bytes 524288
